TPU v7x, 256 devices: a whole 4x4x8 slice. The times are simulated.
256 devices in a mesh: dp: 64 (over z, x, core), mp: 4 (over y).
Axes of the slice: x: 4, y: 4, z: 8, core: 2. Of those that a mesh axis runs over, the one named last changes fastest.
Arguments:
- grad_parts: float32 [64, 2048, 2048], P('dp', None, 'mp'), may hold values from -16 to 16
- master: float32 [2048, 2048], P('dp', 'mp'), may hold values from -0.125 to 0.125
- moment_one: float32 [2048, 2048], P('dp', 'mp'), may hold values from -6 to 6
- moment_two: float32 [2048, 2048], P('dp', 'mp'), may hold values from 0.02 to 0.16
- states: bfloat16 [32768, 2048], P('dp'), may hold values from -6 to 6
- action_ids: int32 [32768, 4], P('dp'), may hold values from 0 to 255
- env_counts: int32 [64], P('dp'), may hold values from 256 to 512, as said below
- owners: int32 [32768, 1], P('dp'), may hold values from 0 to 63; in each aligned block of 512 rows (0 to 511, 512 to 1023, ...) at most 12 rows name the same one
- act_table: bfloat16 [256, 2048], replicated, may hold values from -6 to 6
- norm_gain: float32 [2048], replicated, may hold values from 0.1 to 1.9
- head: bfloat16 [2048, 256], P(None, 'mp'), may hold values from -0.125 to 0.125
Outputs:
- moment_one_new: float32 [2048, 2048], P('dp', 'mp')
- moment_two_new: float32 [2048, 2048], P('dp', 'mp')
- master_new: float32 [2048, 2048], P('dp', 'mp')
- logits: float32 [32768, 256], P('dp', 'mp')
- received: bfloat16 [49152, 2048], P('dp', 'mp')
Inputs may be any that keep to these rules, and one draw needn't show every extreme that they name: `env_counts`: every actor has at least half of its slots live, and some actor has all 512 live. `owners`: among the rows of one actor at most 12 name the same owner, and some actor's rows reach 12 for some owner.
All inputs are finite; a program needn't handle non-finite values.
Results may differ from a plain program's by a relative error of at most 0.017.
Values may be sent and summed in bfloat16 or wider, within the bound.
No kernel may reach another device: no remote copies, remote signals or barrier semaphores. Data moves between devices by JAX's collectives and lax.ppermute only.
A program may use at most 64 MiB of HBM per device.

v0:
```python
import functools

import jax
import jax.numpy as jnp
from jax import lax
from jax.experimental import pallas as pl
from jax.experimental.pallas import tpu as pltpu
from jax.sharding import Mesh, PartitionSpec as P

STEPS = 4
NZ, NX, NC, NY = 8, 4, 2, 4
DP = ("z", "x", "c")
TAGS = 128
VMEM_LIMIT = 60 * 2**20
PARTS = ((0, 0, 4), (1, 0, 4), (3, 0, 4), (2, 0, 2), (2, 2, 2))

beta_one = 0.9
beta_two = 0.999
corr_one = 1.0 - 0.9**10
corr_two = 1.0 - 0.999**10
rate_lr = 0.01
adam_eps = 1e-08
norm_eps = 1e-06
F32 = jnp.float32
BF16 = jnp.bfloat16


def exchange(v, axis):
    return lax.all_to_all(v, axis, 0, 0, tiled=True)


def shift(v, axis, k, n):
    if k == 0:
        return v
    return lax.ppermute(v, axis, [(i, (i + k) % n) for i in range(n)])


def swap(v):
    return shift(v, "c", 1, NC)


def core_rows_kernel(add, core, g_ref, *refs):
    if add:
        got_ref, refs = refs[0], refs[1:]
    out_ref, part, got, done, in_sems, got_sems, out_sems = refs
    nx = part.shape[0]
    loads, extra, stores = [], [], []
    for i in range(nx):
        loads.append(pltpu.make_async_copy(g_ref.at[:, i, core[0]], part.at[i], in_sems.at[i]))
        loads[-1].start()
        if add:
            extra.append(pltpu.make_async_copy(got_ref.at[i], got.at[i], got_sems.at[i]))
            extra[-1].start()
    for i in range(nx):
        loads[i].wait()
        if add:
            extra[i].wait()
            done[i] = (part[i] + got[i].astype(F32)).astype(BF16)
        else:
            done[i] = part[i].astype(BF16)
        stores.append(pltpu.make_async_copy(done.at[i], out_ref.at[i], out_sems.at[i]))
        stores[-1].start()
    for store in stores:
        store.wait()


def core_rows(core, g, *got):
    nz, nx, _, rows, cols = g.shape
    hbm = pl.BlockSpec(memory_space=pl.ANY)
    return pl.pallas_call(
        functools.partial(core_rows_kernel, bool(got)),
        in_specs=[pl.BlockSpec(memory_space=pltpu.SMEM), hbm] + [hbm for _ in got],
        out_specs=hbm,
        out_shape=jax.ShapeDtypeStruct((nx, nz, rows, cols), BF16),
        scratch_shapes=[
            pltpu.VMEM((nx, nz, rows, cols), F32),
            pltpu.VMEM((nx, nz, rows, cols), BF16),
            pltpu.VMEM((nx, nz, rows, cols), BF16),
            pltpu.SemaphoreType.DMA((nx,)),
            pltpu.SemaphoreType.DMA((nx,)),
            pltpu.SemaphoreType.DMA((nx,)),
        ],
        compiler_params=pltpu.CompilerParams(vmem_limit_bytes=VMEM_LIMIT),
    )(core[None].astype(jnp.int32), g, *got)


def decode_kernel(width, place, slots_ref, envs_ref, table_ref, gain_ref, *refs):
    n_pieces = 2 * len(PARTS) * NC
    heads, refs = refs[:NY], refs[NY:]
    pieces, (out_ref, w_ref, hidden, mixed, state, sems) = refs[:n_pieces], refs[n_pieces:]
    my_x, my_c, my_y = place[0], place[1], place[2]
    blocks, wide = w_ref.shape[0], w_ref.shape[-1]
    slots, own = slots_ref.shape[0], envs_ref.shape[0]
    m = slots + own
    tail = out_ref.shape[1] - slots
    copies = ([], [])
    for p in range(n_pieces):
        second, rest = divmod(p, len(PARTS) * NC)
        (k, begin, count), other = PARTS[rest // NC], rest % NC
        core = lax.rem(my_c + other, NC)
        for i in range(begin, begin + count):
            x_off, y_off = (k, i) if second else (i, k)
            x = lax.rem(my_x - x_off + NX, NX)
            y = lax.rem(my_y - y_off + NY, NY)
            copy = pltpu.make_async_copy(
                pieces[p].at[i - begin],
                w_ref.at[2 * y + second, :, x, core],
                sems.at[((second * NX + k) * NX + i) * NC + other],
            )
            copy.start()
            copies[second].append(copy)

    actions = table_ref.shape[0]
    number = lax.broadcasted_iota(jnp.int32, (m, actions), 1) + 1
    lanes = 128

    def onehot(step):
        tags = [ref[:, width:].astype(F32) for ref in (slots_ref, envs_ref)]
        tags = jnp.concatenate(tags, 0)
        chosen = lax.broadcasted_iota(jnp.int32, tags.shape, 1) == step
        tag = jnp.sum(jnp.where(chosen, tags, 0.0), axis=1, keepdims=True).astype(jnp.int32)
        return jnp.where(tag == number, 1.0, 0.0).astype(BF16)

    def embed(hot, cols, old):
        embedded = jnp.dot(hot, table_ref[:, cols], preferred_element_type=F32)
        hidden[:, cols] = (old.astype(F32) + embedded).astype(BF16)

    hot = onehot(0)
    for n in range(blocks):
        cols = slice(n * wide, (n + 1) * wide)
        state[:slots, cols] = slots_ref[:, cols]
        state[slots:, cols] = envs_ref[:, cols]
        embed(hot, cols, state[:, cols])
    for copy in copies[0] + copies[1]:
        copy.wait()

    def control_step(step, carry):
        total = jnp.zeros((m, lanes), F32)
        for n in range(blocks):
            w = w_ref[n].reshape(width, wide)
            got = jnp.dot(hidden[...], w, preferred_element_type=F32).astype(BF16)
            mixed[:, n * wide : (n + 1) * wide] = got
            got = got.astype(F32)
            for at in range(0, wide, lanes):
                total = total + got[:, at : at + lanes] * got[:, at : at + lanes]
        total = jnp.sum(total, axis=1, keepdims=True)
        inverse = lax.rsqrt(total * (1.0 / width) + norm_eps)
        hot = onehot(step + 1)
        for n in range(blocks):
            cols = slice(n * wide, (n + 1) * wide)
            old = state[:, cols].astype(F32)
            new = old + gain_ref[:, cols] * mixed[:, cols].astype(F32) * inverse
            new = new.astype(BF16)
            state[:, cols] = new
            embed(hot, cols, new)
        return carry

    lax.fori_loop(0, STEPS, control_step, 0)
    for y in range(NY):
        out_ref[y, :slots, :] = state[:slots, 2 * y * wide : 2 * (y + 1) * wide]
    for k in range(NY):
        scores = lax.dot_general(
            state[slots:m, :],
            heads[k][...],
            (((1,), (1,)), ((), ())),
            preferred_element_type=F32,
        )
        row = my_y * own + lax.broadcasted_iota(jnp.int32, scores.shape, 0)
        scores = (scores * jnp.where(row < place[3], 1.0, 0.0)).astype(BF16)
        packed = [scores[i * tail : (i + 1) * tail] for i in range(own // tail)]
        out_ref[lax.rem(my_y + k, NY), slots:, :] = jnp.concatenate(packed, 1)


def decode(place, slot_rows, env_rows, table, gain, heads, pieces):
    slots, own, width = slot_rows.shape[0], env_rows.shape[0], table.shape[1]
    wide, m = width // NY // 2, slots + own
    tail = own * heads[0].shape[0] // (width // NY)
    vmem = pl.BlockSpec(memory_space=pltpu.VMEM)
    return pl.pallas_call(
        functools.partial(decode_kernel, width),
        in_specs=[pl.BlockSpec(memory_space=pltpu.SMEM)]
        + [vmem] * (4 + NY)
        + [pl.BlockSpec(memory_space=pl.ANY)] * len(pieces),
        out_specs=vmem,
        out_shape=jax.ShapeDtypeStruct((NY, slots + tail, width // NY), BF16),
        scratch_shapes=[
            pltpu.VMEM((2 * NY, NZ, NX, NC, width // (NZ * NX * NC), wide), BF16),
            pltpu.VMEM((m, width), BF16),
            pltpu.VMEM((m, width), BF16),
            pltpu.VMEM((m, width), BF16),
            pltpu.SemaphoreType.DMA((2 * NX * NX * NC,)),
        ],
        compiler_params=pltpu.CompilerParams(vmem_limit_bytes=VMEM_LIMIT),
        cost_estimate=pl.CostEstimate(
            flops=2 * STEPS * m * width * width, bytes_accessed=2 * width * width, transcendentals=0
        ),
    )(place, slot_rows, env_rows, table, gain, *heads, *pieces)


def body(
    grad_parts,
    master,
    moment_one,
    moment_two,
    states,
    action_ids,
    env_counts,
    owners,
    act_table,
    norm_gain,
    head,
):
    width, cols = grad_parts.shape[1:]
    rows = width // (NZ * NX * NC)
    half = cols // 2
    env_slots = states.shape[0]
    owner_num = NZ * NX * NC
    capacity = max(2, 3 * env_slots // (2 * owner_num))
    share = capacity // NY
    slots = owner_num * share
    own = env_slots // NY
    my_x, my_c, my_y = lax.axis_index("x"), lax.axis_index("c"), lax.axis_index("y")
    place = jnp.stack([my_x, my_c, my_y, env_counts[0]]).astype(jnp.int32)

    g = grad_parts[0].reshape(NZ, NX, NC, rows, cols)
    both = core_rows(my_c, g, swap(core_rows(1 - my_c, g)))
    both, head = lax.optimization_barrier((both, head))
    by_x = exchange(both, "x")
    head = head.T
    heads = [head, shift(head, "y", 3, NY), None, shift(head, "y", 1, NY)]
    by_x, heads[1], heads[3], states, head = lax.optimization_barrier(
        (by_x, heads[1], heads[3], states, head)
    )
    heads[2] = shift(head, "y", 2, NY)
    by_x = by_x.astype(F32).sum(0).astype(BF16)
    gradient = exchange(by_x, "z").astype(F32).sum(0)

    active = jnp.arange(env_slots, dtype=jnp.int32) < env_counts[0]
    target = owners[:, 0]
    marks = (
        (target[:, None] == jnp.arange(owner_num, dtype=jnp.int32)[None, :]) & active[:, None]
    ).astype(jnp.int32)
    ranked = jnp.cumsum(marks, axis=0) - marks
    slot_idx = jnp.sum(ranked * marks, axis=1)
    mine = active & (slot_idx // share == my_y)
    column = target // NC % NX
    ahead = lax.rem(column - my_x + NX, NX)
    group = target // (NC * NX) * NC + target % NC
    groups = NZ * NC
    index = jnp.where(mine, (ahead * groups + group - my_y) * share + slot_idx, -1)
    pick = (jnp.arange(slots, dtype=jnp.int32)[:, None] == index[None, :]).astype(BF16)
    tags = jnp.pad((action_ids + 1).astype(BF16), ((0, 0), (0, TAGS - STEPS)))
    tagged = jnp.concatenate([states, tags], 1)
    outgoing = jnp.dot(pick, tagged, preferred_element_type=F32).astype(BF16)
    span = groups * share
    outgoing = [shift(outgoing[k * span : (k + 1) * span], "x", k, NX) for k in range(NX)]
    deep = -(-NX * share // 16) * 16
    row = jnp.arange(groups * deep, dtype=jnp.int32)
    place_in, part = row % deep, row // deep
    from_row = place_in // share * span + part * share + place_in % share
    from_row = jnp.where(place_in < NX * share, from_row, -1)
    pick = (from_row[:, None] == jnp.arange(slots, dtype=jnp.int32)[None, :]).astype(BF16)
    outgoing = jnp.dot(pick, jnp.concatenate(outgoing, 0), preferred_element_type=F32)
    outgoing = outgoing.astype(BF16).reshape(groups, deep, width + TAGS)
    actor_rows = lax.dynamic_slice_in_dim(tagged, my_y * own, own, 0)

    m_new = beta_one * moment_one + (1.0 - beta_one) * gradient
    v_new = beta_two * moment_two + (1.0 - beta_two) * gradient * gradient
    w_new = master - rate_lr * (m_new / corr_one) / (jnp.sqrt(v_new / corr_two) + adam_eps)

    w = exchange(jnp.broadcast_to(w_new.astype(BF16)[None], (NZ, rows, cols)), "z")
    w, outgoing, actor_rows, heads = lax.optimization_barrier((w, outgoing, actor_rows, heads))
    first, second = w[..., :half], w[..., half:]
    first = jnp.stack([shift(first, "x", k, NX) for k in range(NX)])
    second = jnp.stack([shift(second, "y", k, NY) for k in range(NY)])
    arrived = exchange(outgoing, ("z", "c")).reshape(groups * deep, width + TAGS)
    row = jnp.arange(slots, dtype=jnp.int32)
    source, behind = row // share, lax.rem(my_x - row // share // NC % NX + NX, NX)
    from_row = (source // (NC * NX) * NC + source % NC) * deep + behind * share + row % share
    pick = (from_row[:, None] == jnp.arange(groups * deep, dtype=jnp.int32)[None, :]).astype(BF16)
    slot_rows = jnp.dot(pick, arrived, preferred_element_type=F32).astype(BF16)
    first, second = lax.optimization_barrier((first, second))
    near = [shift(v, axis, k, NX) for v, axis in ((first, "y"), (second, "x")) for k in (1, 3)]
    near = lax.optimization_barrier(near)
    far = []
    for (back, front), axis in ((near[:2], "y"), (near[2:], "x")):
        far += [shift(back[: NX // 2], axis, 1, NX), shift(front[NX // 2 :], axis, 3, NX)]
    far, slot_rows = lax.optimization_barrier((far, slot_rows))
    pieces = []
    for piece in [first, *near[:2], *far[:2], second, *near[2:], *far[2:]]:
        pieces += [piece, swap(piece)]

    final = decode(place, slot_rows, actor_rows, act_table, norm_gain[None, :], heads, pieces)
    landed = exchange(final, "y")

    each = head.shape[0]
    scores = landed[:, slots:].astype(F32).reshape(NY, -1, cols // each, each)
    logits = jnp.transpose(scores, (0, 2, 1, 3)).reshape(env_slots, each)

    row = jnp.arange(owner_num * capacity, dtype=jnp.int32)
    at = row % capacity // share * slots + row // capacity * share + row % share
    order = (at[:, None] == row[None, :]).astype(BF16)
    landed = landed[:, :slots].reshape(owner_num * capacity, cols)
    received = jnp.dot(order, landed, preferred_element_type=F32)
    return (m_new, v_new, w_new, logits, received.astype(BF16))


def solution(mesh):
    grid = Mesh(mesh.devices.reshape(NZ, NX, NC, NY), DP + ("y",))
    in_specs = (
        P(DP, None, "y"),
        P(DP, "y"),
        P(DP, "y"),
        P(DP, "y"),
        P(DP, None),
        P(DP, None),
        P(DP),
        P(DP, None),
        P(),
        P(),
        P(None, "y"),
    )
    out_specs = (P(DP, "y"),) * 5
    return jax.shard_map(body, mesh=grid, in_specs=in_specs, out_specs=out_specs, check_vma=False)
```

profile of v0, /device:TPU:1, one launch (start us, length us, event | category | flops | bytes accessed | tf_op | source)
XLA Modules:
  0.0 164.9 jit_solution(264524293588659162)
XLA Ops:
  0.6 2.4 %shard_map.146 = bf16[4,8,32,512]{3,2,1,0:T(8,128)(2,1)} custom-call(s32[1]{0:T(128)} %bitcast.2.core, f32[8,4,2,32,512]{4,3,2,1,0:T(8,128)} %bitcast.50), custom_call_target="tpu_custom_call" | custom-call | tf_op jit(solution)/shard_map/pallas_call | solution.py:70
  3.0 3.3 %collective-permute-start = (bf16[4,8,32,512]{3,2,1,0:T(8,128)(2,1)}, bf16[4,8,32,512]{3,2,1,0:T(8,128)(2,1)S(1)}, u32[]{:S(2)}, u32[]{:S(2)}) collective-permute-start(bf16[4,8,32,512]{3,2,1,0:T(8,128)(2,1)} %shard_map.146), channel_id=1, source_target_pairs={{0,4},{4,0},{1,5},{5,1},{2,6},{6,2},{3,7},{7,3},{8,12},{12,8},{9,1... | collective-permute-start | bytes 3145736 | tf_op jit(solution)/shard_map/ppermute | solution.py:35
  9.8 2.7 %shard_map.147 = bf16[4,8,32,512]{3,2,1,0:T(8,128)(2,1)} custom-call(s32[1]{0:T(128)} %bitcast.core, f32[8,4,2,32,512]{4,3,2,1,0:T(8,128)} %bitcast.51, bf16[4,8,32,512]{3,2,1,0:T(8,128)(2,1)} %copy-done.2), custom_call_target="tpu_custom_call" | custom-call | tf_op jit(solution)/shard_map/pallas_call | solution.py:70
  12.5 3.7 %all-to-all-start = ((bf16[4,8,32,512]{3,2,1,0:T(8,128)(2,1)}), bf16[4,8,32,512]{3,2,1,0:T(8,128)(2,1)S(1)}, u32[]{:S(2)}, u32[]{:S(2)}) async-start(bf16[4,8,32,512]{3,2,1,0:T(8,128)(2,1)} %shard_map.147), calls=%async_computation | async-start | bytes 2097152 | tf_op jit(solution)/shard_map/all_to_all | solution.py:29
  16.3 1.6 collective-permute-start.1
  18.1 6.1 %collective-permute-done.1.refs_1_ = bf16[64,2048]{1,0:T(8,128)(2,1)} collective-permute-done((bf16[64,2048]{1,0:T(8,128)(2,1)}, bf16[64,2048]{1,0:T(8,128)(2,1)}, u32[]{:S(2)}, u32[]{:S(2)}) %collective-permute-start.1) | collective-permute-done | bytes 262176 | tf_op jit(solution)/shard_map/ppermute | solution.py:35
  24.3 2.0 %collective-permute-done.2.refs_3_ = bf16[64,2048]{1,0:T(8,128)(2,1)} collective-permute-done((bf16[64,2048]{1,0:T(8,128)(2,1)}, bf16[64,2048]{1,0:T(8,128)(2,1)}, u32[]{:S(2)}, u32[]{:S(2)}) %collective-permute-start.2) | collective-permute-done | bytes 262176 | tf_op jit(solution)/shard_map/ppermute | solution.py:35
  26.3 4.7 %all-to-all-done = bf16[4,8,32,512]{3,2,1,0:T(8,128)(2,1)S(1)} async-done(((bf16[4,8,32,512]{3,2,1,0:T(8,128)(2,1)}), bf16[4,8,32,512]{3,2,1,0:T(8,128)(2,1)S(1)}, u32[]{:S(2)}, u32[]{:S(2)}) %all-to-all-start) | async-done | bytes 1048608 | tf_op jit(solution)/shard_map/all_to_all | solution.py:29
  31.9 6.7 %all-to-all-start.1 = ((bf16[8,32,512]{2,1,0:T(8,128)(2,1)}), bf16[8,32,512]{2,1,0:T(8,128)(2,1)S(1)}, u32[]{:S(2)}, u32[]{:S(2)}) async-start(bf16[8,32,512]{2,1,0:T(8,128)(2,1)} %reduce_sum.30), calls=%async_computation.1 | async-start | bytes 524288 | tf_op jit(solution)/shard_map/all_to_all | solution.py:29
  42.1 2.9 %collective-permute-start.6 = (bf16[64,2048]{1,0:T(8,128)(2,1)}, bf16[64,2048]{1,0:T(8,128)(2,1)}, u32[]{:S(2)}, u32[]{:S(2)}) collective-permute-start(bf16[64,2048]{1,0:T(8,128)(2,1)} %bitcast.3.refs_0_), channel_id=1, source_target_pairs={{0,2},{1,3},{2,0},{3,1},{4,6},{5,7},{6,4},{7,5},{8,10},{9,11},{10,... | collective-permute-start | bytes 786440 | tf_op jit(solution)/shard_map/ppermute | solution.py:35
  45.2 2.9 %all-to-all-done.1 = bf16[8,32,512]{2,1,0:T(8,128)(2,1)S(1)} async-done(((bf16[8,32,512]{2,1,0:T(8,128)(2,1)}), bf16[8,32,512]{2,1,0:T(8,128)(2,1)S(1)}, u32[]{:S(2)}, u32[]{:S(2)}) %all-to-all-start.1) | async-done | bytes 262176 | tf_op jit(solution)/shard_map/all_to_all | solution.py:29
  50.4 3.8 %all-to-all-start.2 = ((bf16[8,32,512]{2,1,0:T(8,128)(2,1)}), bf16[8,32,512]{2,1,0:T(8,128)(2,1)S(1)}, u32[]{:S(2)}, u32[]{:S(2)}) async-start(bf16[8,32,512]{2,1,0:T(8,128)(2,1)} %broadcast_in_dim.14), calls=%async_computation.2 | async-start | bytes 524288 | tf_op jit(solution)/shard_map/all_to_all | solution.py:29
  55.0 2.7 %convolution_convert_fusion = bf16[256,2176]{1,0:T(8,128)(2,1)} fusion(bf16[48,2176]{1,0:T(8,128)(2,1)} %collective-permute-done.5, bf16[48,2176]{1,0:T(8,128)(2,1)} %collective-permute-done.4, bf16[48,2176]{1,0:T(8,128)(2,1)} %collective-permute-done.3, bf16[48,2176]{1,0:T(8,128)(2,1)S(1)} %get-tuple-element.74, s32[256]{0:T(256)S(1)} %compare_select_fusion.4), kind=kOutput, calls=%fused_computation.2 | convolution fusion | flops 217858048 | bytes 1950720 | tf_op jit(solution)/shard_map/dot_general | solution.py:263
  57.7 5.9 %all-to-all-done.2 = bf16[8,32,512]{2,1,0:T(8,128)(2,1)S(1)} async-done(((bf16[8,32,512]{2,1,0:T(8,128)(2,1)}), bf16[8,32,512]{2,1,0:T(8,128)(2,1)S(1)}, u32[]{:S(2)}, u32[]{:S(2)}) %all-to-all-start.2) | async-done | bytes 262176 | tf_op jit(solution)/shard_map/all_to_all | solution.py:29
  63.6 7.7 %all-to-all-start.3 = ((bf16[16,16,2176]{2,1,0:T(8,128)(2,1)}), bf16[16,16,2176]{2,1,0:T(8,128)(2,1)S(1)}, u32[]{:S(2)}, u32[]{:S(2)}) async-start(bf16[16,16,2176]{2,1,0:T(8,128)(2,1)} %bitcast.10), calls=%async_computation.3 | async-start | bytes 2228224 | tf_op jit(solution)/shard_map/all_to_all | solution.py:29
  71.4 3.0 %collective-permute-start.9 = (bf16[8,32,256]{2,1,0:T(8,128)(2,1)S(1)}, bf16[8,32,256]{2,1,0:T(8,128)(2,1)S(1)}, u32[]{:S(2)}, u32[]{:S(2)}) collective-permute-start(bf16[8,32,256]{2,1,0:T(8,128)(2,1)S(1)} %get-tuple-element.81), channel_id=1, source_target_pairs={{0,24},{8,0},{16,8},{24,16},{1,25},{9,1},{17,9},{25,17},{2,26},{10... | collective-permute-start | bytes 393224 | tf_op jit(solution)/shard_map/ppermute | solution.py:35
  77.7 2.0 %collective-permute-done.9 = bf16[8,32,256]{2,1,0:T(8,128)(2,1)S(1)} collective-permute-done((bf16[8,32,256]{2,1,0:T(8,128)(2,1)S(1)}, bf16[8,32,256]{2,1,0:T(8,128)(2,1)S(1)}, u32[]{:S(2)}, u32[]{:S(2)}) %collective-permute-start.9) | collective-permute-done | bytes 131104 | tf_op jit(solution)/shard_map/ppermute | solution.py:35
  80.5 3.7 %collective-permute-done.7 = bf16[8,32,256]{2,1,0:T(8,128)(2,1)S(1)} collective-permute-done((bf16[8,32,256]{2,1,0:T(8,128)(2,1)S(1)}, bf16[8,32,256]{2,1,0:T(8,128)(2,1)S(1)}, u32[]{:S(2)}, u32[]{:S(2)}) %collective-permute-start.7) | collective-permute-done | bytes 131104 | tf_op jit(solution)/shard_map/ppermute | solution.py:35
  84.2 2.1 %collective-permute-done.10 = bf16[8,32,256]{2,1,0:T(8,128)(2,1)S(1)} collective-permute-done((bf16[8,32,256]{2,1,0:T(8,128)(2,1)S(1)}, bf16[8,32,256]{2,1,0:T(8,128)(2,1)S(1)}, u32[]{:S(2)}, u32[]{:S(2)}) %collective-permute-start.10) | collective-permute-done | bytes 131104 | tf_op jit(solution)/shard_map/ppermute | solution.py:35
  86.5 2.7 %collective-permute-start.14 = (bf16[4,8,32,256]{3,2,1,0:T(8,128)(2,1)S(1)}, bf16[4,8,32,256]{3,2,1,0:T(8,128)(2,1)S(1)}, u32[]{:S(2)}, u32[]{:S(2)}) collective-permute-start(bf16[4,8,32,256]{3,2,1,0:T(8,128)(2,1)S(1)} %pad_maximum_fusion.refs_4_), channel_id=1, source_target_pairs={{0,3},{1,0},{2,1},{3,2},{4,7},{5,4},{6,5},{7,6},{8,11},{9,8},{10,9... | collective-permute-start | bytes 1572872 | tf_op jit(solution)/shard_map/ppermute | solution.py:35
  89.3 2.5 %collective-permute-start.16 = (bf16[4,8,32,256]{3,2,1,0:T(8,128)(2,1)S(1)}, bf16[4,8,32,256]{3,2,1,0:T(8,128)(2,1)}, u32[]{:S(2)}, u32[]{:S(2)}) collective-permute-start(bf16[4,8,32,256]{3,2,1,0:T(8,128)(2,1)S(1)} %pad_maximum_fusion.1.refs_14_), channel_id=1, source_target_pairs={{0,24},{8,0},{16,8},{24,16},{1,25},{9,1},{17,9},{25,17},{2,26},{10... | collective-permute-start | bytes 1572872 | tf_op jit(solution)/shard_map/ppermute | solution.py:35
  91.8 2.4 %collective-permute-start.21 = (bf16[4,8,32,256]{3,2,1,0:T(8,128)(2,1)S(1)}, bf16[4,8,32,256]{3,2,1,0:T(8,128)(2,1)S(1)}, u32[]{:S(2)}, u32[]{:S(2)}) collective-permute-start(bf16[4,8,32,256]{3,2,1,0:T(8,128)(2,1)S(1)} %pad_maximum_fusion.refs_4_), channel_id=1, source_target_pairs={{0,4},{4,0},{1,5},{5,1},{2,6},{6,2},{3,7},{7,3},{8,12},{12,8},{9,1... | collective-permute-start | bytes 1572872 | tf_op jit(solution)/shard_map/ppermute | solution.py:35
  94.3 5.6 %collective-permute-done.13.refs_6_ = bf16[4,8,32,256]{3,2,1,0:T(8,128)(2,1)S(1)} collective-permute-done((bf16[4,8,32,256]{3,2,1,0:T(8,128)(2,1)S(1)}, bf16[4,8,32,256]{3,2,1,0:T(8,128)(2,1)S(1)}, u32[]{:S(2)}, u32[]{:S(2)}) %collective-permute-start.13) | collective-permute-done | bytes 524320 | tf_op jit(solution)/shard_map/ppermute | solution.py:35
  99.9 2.1 %collective-permute-done.15.refs_16_ = bf16[4,8,32,256]{3,2,1,0:T(8,128)(2,1)} collective-permute-done((bf16[4,8,32,256]{3,2,1,0:T(8,128)(2,1)S(1)}, bf16[4,8,32,256]{3,2,1,0:T(8,128)(2,1)}, u32[]{:S(2)}, u32[]{:S(2)}) %collective-permute-start.15) | collective-permute-done | bytes 524320 | tf_op jit(solution)/shard_map/ppermute | solution.py:35
  102.1 2.7 %collective-permute-start.18 = (bf16[2,8,32,256]{3,2,1,0:T(8,128)(2,1)S(1)}, bf16[2,8,32,256]{3,2,1,0:T(8,128)(2,1)S(1)}, u32[]{:S(2)}, u32[]{:S(2)}) collective-permute-start(bf16[2,8,32,256]{3,2,1,0:T(8,128)(2,1)S(1)} %slice.51), channel_id=1, source_target_pairs={{0,3},{1,0},{2,1},{3,2},{4,7},{5,4},{6,5},{7,6},{8,11},{9,8},{10,9... | collective-permute-start | bytes 786440 | tf_op jit(solution)/shard_map/ppermute | solution.py:35
  106.9 2.7 %collective-permute-start.20 = (bf16[2,8,32,256]{3,2,1,0:T(8,128)(2,1)S(1)}, bf16[2,8,32,256]{3,2,1,0:T(8,128)(2,1)S(1)}, u32[]{:S(2)}, u32[]{:S(2)}) collective-permute-start(bf16[2,8,32,256]{3,2,1,0:T(8,128)(2,1)S(1)} %slice.53), channel_id=1, source_target_pairs={{0,24},{8,0},{16,8},{24,16},{1,25},{9,1},{17,9},{25,17},{2,26},{10... | collective-permute-start | bytes 786440 | tf_op jit(solution)/shard_map/ppermute | solution.py:35
  109.7 3.9 %collective-permute-start.26 = (bf16[4,8,32,256]{3,2,1,0:T(8,128)(2,1)S(1)}, bf16[4,8,32,256]{3,2,1,0:T(8,128)(2,1)}, u32[]{:S(2)}, u32[]{:S(2)}) collective-permute-start(bf16[4,8,32,256]{3,2,1,0:T(8,128)(2,1)S(1)} %pad_maximum_fusion.1.refs_14_), channel_id=1, source_target_pairs={{0,4},{4,0},{1,5},{5,1},{2,6},{6,2},{3,7},{7,3},{8,12},{12,8},{9,1... | collective-permute-start | bytes 1572872 | tf_op jit(solution)/shard_map/ppermute | solution.py:35
  114.1 2.8 %collective-permute-start.27 = (bf16[4,8,32,256]{3,2,1,0:T(8,128)(2,1)}, bf16[4,8,32,256]{3,2,1,0:T(8,128)(2,1)}, u32[]{:S(2)}, u32[]{:S(2)}) collective-permute-start(bf16[4,8,32,256]{3,2,1,0:T(8,128)(2,1)} %collective-permute-done.15.refs_16_), channel_id=1, source_target_pairs={{0,4},{4,0},{1,5},{5,1},{2,6},{6,2},{3,7},{7,3},{8,12},{12,8},{9,1... | collective-permute-start | bytes 1572872 | tf_op jit(solution)/shard_map/ppermute | solution.py:35
  123.2 22.5 %shard_map.148 = bf16[4,208,512]{2,1,0:T(8,128)(2,1)} custom-call(s32[4]{0:T(128)} %pad_add_fusion.place, bf16[192,2176]{1,0:T(8,128)(2,1)} %convolution_convert_fusion.1.slots_ref, bf16[128,2176]{1,0:T(8,128)(2,1)} %constant_dynamic-slice_fusion.envs_ref, bf16[256,2048]{1,0:T(8,128)(2,1)} %table_ref.1, f32[1,2048]{1,0:T(1,128)} %bitcast.64, ...), custom_call_target="tpu_custom_call" | custom-call | flops 10737418240 | bytes 8388608 | tf_op jit(solution)/shard_map/pallas_call | solution.py:179
  145.7 3.5 %all-to-all-start.4 = ((bf16[4,208,512]{2,1,0:T(8,128)(2,1)}), bf16[4,208,512]{2,1,0:T(8,128)(2,1)S(1)}, u32[]{:S(2)}, u32[]{:S(2)}) async-start(bf16[4,208,512]{2,1,0:T(8,128)(2,1)} %shard_map.148), calls=%async_computation.4 | async-start | bytes 1703936 | tf_op jit(solution)/shard_map/all_to_all | solution.py:29
  149.3 12.9 %all-to-all-done.4 = bf16[4,208,512]{2,1,0:T(8,128)(2,1)S(1)} async-done(((bf16[4,208,512]{2,1,0:T(8,128)(2,1)}), bf16[4,208,512]{2,1,0:T(8,128)(2,1)S(1)}, u32[]{:S(2)}, u32[]{:S(2)}) %all-to-all-start.4) | async-done | bytes 852000 | tf_op jit(solution)/shard_map/all_to_all | solution.py:29
  163.2 1.7 %fusion.3 = bf16[768,512]{1,0:T(8,128)(2,1)} fusion(bf16[768,512]{1,0:T(8,128)(2,1)S(1)} %bitcast.54, s32[768]{0:T(1024)S(1)} %fusion.34), kind=kOutput, calls=%fused_computation.8 | convolution fusion | flops 604962816 | bytes 1575936 | tf_op jit(solution)/shard_map/dot_general | solution.py:304
  (121 shorter events, 25.3 us)
Async XLA Ops:
  3.0 5.8 %collective-permute-start = (bf16[4,8,32,512]{3,2,1,0:T(8,128)(2,1)}, bf16[4,8,32,512]{3,2,1,0:T(8,128)(2,1)S(1)}, u32[]{:S(2)}, u32[]{:S(2)}) collective-permute-start(bf16[4,8,32,512]{3,2,1,0:T(8,128)(2,1)} %shard_map.146), channel_id=1, source_target_pairs={{0,4},{4,0},{1,5},{5,1},{2,6},{6,2},{3,7},{7,3},{8,12},{12,8},{9,1... | collective-permute-start | bytes 3145736 | tf_op jit(solution)/shard_map/ppermute | solution.py:35
  12.5 18.5 %all-to-all-start = ((bf16[4,8,32,512]{3,2,1,0:T(8,128)(2,1)}), bf16[4,8,32,512]{3,2,1,0:T(8,128)(2,1)S(1)}, u32[]{:S(2)}, u32[]{:S(2)}) async-start(bf16[4,8,32,512]{3,2,1,0:T(8,128)(2,1)} %shard_map.147), calls=%async_computation | async-start | bytes 2097152 | tf_op jit(solution)/shard_map/all_to_all | solution.py:29
  16.3 7.9 %collective-permute-start.1 = (bf16[64,2048]{1,0:T(8,128)(2,1)}, bf16[64,2048]{1,0:T(8,128)(2,1)}, u32[]{:S(2)}, u32[]{:S(2)}) collective-permute-start(bf16[64,2048]{1,0:T(8,128)(2,1)} %bitcast.3.refs_0_), channel_id=1, source_target_pairs={{0,3},{1,0},{2,1},{3,2},{4,7},{5,4},{6,5},{7,6},{8,11},{9,8},{10,9... | collective-permute-start | bytes 786440 | tf_op jit(solution)/shard_map/ppermute | solution.py:35
  17.9 8.4 %collective-permute-start.2 = (bf16[64,2048]{1,0:T(8,128)(2,1)}, bf16[64,2048]{1,0:T(8,128)(2,1)}, u32[]{:S(2)}, u32[]{:S(2)}) collective-permute-start(bf16[64,2048]{1,0:T(8,128)(2,1)} %bitcast.3.refs_0_), channel_id=1, source_target_pairs={{0,1},{1,2},{2,3},{3,0},{4,5},{5,6},{6,7},{7,4},{8,9},{9,10},{10,1... | collective-permute-start | bytes 786440 | tf_op jit(solution)/shard_map/ppermute | solution.py:35
  31.9 16.1 %all-to-all-start.1 = ((bf16[8,32,512]{2,1,0:T(8,128)(2,1)}), bf16[8,32,512]{2,1,0:T(8,128)(2,1)S(1)}, u32[]{:S(2)}, u32[]{:S(2)}) async-start(bf16[8,32,512]{2,1,0:T(8,128)(2,1)} %reduce_sum.30), calls=%async_computation.1 | async-start | bytes 524288 | tf_op jit(solution)/shard_map/all_to_all | solution.py:29
  40.0 15.0 %collective-permute-start.5 = (bf16[48,2176]{1,0:T(8,128)(2,1)}, bf16[48,2176]{1,0:T(8,128)(2,1)}, u32[]{:S(2)}, u32[]{:S(2)}) collective-permute-start(bf16[48,2176]{1,0:T(8,128)(2,1)} %get-tuple-element.75), channel_id=1, source_target_pairs={{0,24},{8,0},{16,8},{24,16},{1,25},{9,1},{17,9},{25,17},{2,26},{10... | collective-permute-start | bytes 626696 | tf_op jit(solution)/shard_map/ppermute | solution.py:35
  40.9 14.1 %collective-permute-start.4 = (bf16[48,2176]{1,0:T(8,128)(2,1)S(1)}, bf16[48,2176]{1,0:T(8,128)(2,1)}, u32[]{:S(2)}, u32[]{:S(2)}) collective-permute-start(bf16[48,2176]{1,0:T(8,128)(2,1)S(1)} %get-tuple-element.76), channel_id=1, source_target_pairs={{0,16},{8,24},{16,0},{24,8},{1,17},{9,25},{17,1},{25,9},{2,18},{10... | collective-permute-start | bytes 626696 | tf_op jit(solution)/shard_map/ppermute | solution.py:35
  42.1 12.9 %collective-permute-start.3 = (bf16[48,2176]{1,0:T(8,128)(2,1)S(1)}, bf16[48,2176]{1,0:T(8,128)(2,1)}, u32[]{:S(2)}, u32[]{:S(2)}) collective-permute-start(bf16[48,2176]{1,0:T(8,128)(2,1)S(1)} %get-tuple-element.77), channel_id=1, source_target_pairs={{0,8},{8,16},{16,24},{24,0},{1,9},{9,17},{17,25},{25,1},{2,10},{10... | collective-permute-start | bytes 626696 | tf_op jit(solution)/shard_map/ppermute | solution.py:35
  42.1 15.6 %collective-permute-start.6 = (bf16[64,2048]{1,0:T(8,128)(2,1)}, bf16[64,2048]{1,0:T(8,128)(2,1)}, u32[]{:S(2)}, u32[]{:S(2)}) collective-permute-start(bf16[64,2048]{1,0:T(8,128)(2,1)} %bitcast.3.refs_0_), channel_id=1, source_target_pairs={{0,2},{1,3},{2,0},{3,1},{4,6},{5,7},{6,4},{7,5},{8,10},{9,11},{10,... | collective-permute-start | bytes 786440 | tf_op jit(solution)/shard_map/ppermute | solution.py:35
  50.4 13.2 %all-to-all-start.2 = ((bf16[8,32,512]{2,1,0:T(8,128)(2,1)}), bf16[8,32,512]{2,1,0:T(8,128)(2,1)S(1)}, u32[]{:S(2)}, u32[]{:S(2)}) async-start(bf16[8,32,512]{2,1,0:T(8,128)(2,1)} %broadcast_in_dim.14), calls=%async_computation.2 | async-start | bytes 524288 | tf_op jit(solution)/shard_map/all_to_all | solution.py:29
  63.6 54.7 %all-to-all-start.3 = ((bf16[16,16,2176]{2,1,0:T(8,128)(2,1)}), bf16[16,16,2176]{2,1,0:T(8,128)(2,1)S(1)}, u32[]{:S(2)}, u32[]{:S(2)}) async-start(bf16[16,16,2176]{2,1,0:T(8,128)(2,1)} %bitcast.10), calls=%async_computation.3 | async-start | bytes 2228224 | tf_op jit(solution)/shard_map/all_to_all | solution.py:29
  71.4 8.4 %collective-permute-start.9 = (bf16[8,32,256]{2,1,0:T(8,128)(2,1)S(1)}, bf16[8,32,256]{2,1,0:T(8,128)(2,1)S(1)}, u32[]{:S(2)}, u32[]{:S(2)}) collective-permute-start(bf16[8,32,256]{2,1,0:T(8,128)(2,1)S(1)} %get-tuple-element.81), channel_id=1, source_target_pairs={{0,24},{8,0},{16,8},{24,16},{1,25},{9,1},{17,9},{25,17},{2,26},{10... | collective-permute-start | bytes 393224 | tf_op jit(solution)/shard_map/ppermute | solution.py:35
  74.4 6.1 %collective-permute-start.8 = (bf16[8,32,256]{2,1,0:T(8,128)(2,1)S(1)}, bf16[8,32,256]{2,1,0:T(8,128)(2,1)S(1)}, u32[]{:S(2)}, u32[]{:S(2)}) collective-permute-start(bf16[8,32,256]{2,1,0:T(8,128)(2,1)S(1)} %get-tuple-element.81), channel_id=1, source_target_pairs={{0,16},{8,24},{16,0},{24,8},{1,17},{9,25},{17,1},{25,9},{2,18},{10... | collective-permute-start | bytes 393224 | tf_op jit(solution)/shard_map/ppermute | solution.py:35
  75.0 9.2 %collective-permute-start.7 = (bf16[8,32,256]{2,1,0:T(8,128)(2,1)S(1)}, bf16[8,32,256]{2,1,0:T(8,128)(2,1)S(1)}, u32[]{:S(2)}, u32[]{:S(2)}) collective-permute-start(bf16[8,32,256]{2,1,0:T(8,128)(2,1)S(1)} %get-tuple-element.81), channel_id=1, source_target_pairs={{0,8},{8,16},{16,24},{24,0},{1,9},{9,17},{17,25},{25,1},{2,10},{10... | collective-permute-start | bytes 393224 | tf_op jit(solution)/shard_map/ppermute | solution.py:35
  75.5 8.7 %collective-permute-start.12 = (bf16[8,32,256]{2,1,0:T(8,128)(2,1)S(1)}, bf16[8,32,256]{2,1,0:T(8,128)(2,1)S(1)}, u32[]{:S(2)}, u32[]{:S(2)}) collective-permute-start(bf16[8,32,256]{2,1,0:T(8,128)(2,1)S(1)} %get-tuple-element.80), channel_id=1, source_target_pairs={{0,3},{1,0},{2,1},{3,2},{4,7},{5,4},{6,5},{7,6},{8,11},{9,8},{10,9... | collective-permute-start | bytes 393224 | tf_op jit(solution)/shard_map/ppermute | solution.py:35
  76.3 7.9 %collective-permute-start.11 = (bf16[8,32,256]{2,1,0:T(8,128)(2,1)S(1)}, bf16[8,32,256]{2,1,0:T(8,128)(2,1)S(1)}, u32[]{:S(2)}, u32[]{:S(2)}) collective-permute-start(bf16[8,32,256]{2,1,0:T(8,128)(2,1)S(1)} %get-tuple-element.80), channel_id=1, source_target_pairs={{0,2},{1,3},{2,0},{3,1},{4,6},{5,7},{6,4},{7,5},{8,10},{9,11},{10,... | collective-permute-start | bytes 393224 | tf_op jit(solution)/shard_map/ppermute | solution.py:35
  79.7 6.6 %collective-permute-start.10 = (bf16[8,32,256]{2,1,0:T(8,128)(2,1)S(1)}, bf16[8,32,256]{2,1,0:T(8,128)(2,1)S(1)}, u32[]{:S(2)}, u32[]{:S(2)}) collective-permute-start(bf16[8,32,256]{2,1,0:T(8,128)(2,1)S(1)} %get-tuple-element.80), channel_id=1, source_target_pairs={{0,1},{1,2},{2,3},{3,0},{4,5},{5,6},{6,7},{7,4},{8,9},{9,10},{10,1... | collective-permute-start | bytes 393224 | tf_op jit(solution)/shard_map/ppermute | solution.py:35
  86.4 13.5 %collective-permute-start.13 = (bf16[4,8,32,256]{3,2,1,0:T(8,128)(2,1)S(1)}, bf16[4,8,32,256]{3,2,1,0:T(8,128)(2,1)S(1)}, u32[]{:S(2)}, u32[]{:S(2)}) collective-permute-start(bf16[4,8,32,256]{3,2,1,0:T(8,128)(2,1)S(1)} %pad_maximum_fusion.refs_4_), channel_id=1, source_target_pairs={{0,1},{1,2},{2,3},{3,0},{4,5},{5,6},{6,7},{7,4},{8,9},{9,10},{10,1... | collective-permute-start | bytes 1572872 | tf_op jit(solution)/shard_map/ppermute | solution.py:35
  86.5 13.4 %collective-permute-start.14 = (bf16[4,8,32,256]{3,2,1,0:T(8,128)(2,1)S(1)}, bf16[4,8,32,256]{3,2,1,0:T(8,128)(2,1)S(1)}, u32[]{:S(2)}, u32[]{:S(2)}) collective-permute-start(bf16[4,8,32,256]{3,2,1,0:T(8,128)(2,1)S(1)} %pad_maximum_fusion.refs_4_), channel_id=1, source_target_pairs={{0,3},{1,0},{2,1},{3,2},{4,7},{5,4},{6,5},{7,6},{8,11},{9,8},{10,9... | collective-permute-start | bytes 1572872 | tf_op jit(solution)/shard_map/ppermute | solution.py:35
  89.2 12.9 %collective-permute-start.15 = (bf16[4,8,32,256]{3,2,1,0:T(8,128)(2,1)S(1)}, bf16[4,8,32,256]{3,2,1,0:T(8,128)(2,1)}, u32[]{:S(2)}, u32[]{:S(2)}) collective-permute-start(bf16[4,8,32,256]{3,2,1,0:T(8,128)(2,1)S(1)} %pad_maximum_fusion.1.refs_14_), channel_id=1, source_target_pairs={{0,8},{8,16},{16,24},{24,0},{1,9},{9,17},{17,25},{25,1},{2,10},{10... | collective-permute-start | bytes 1572872 | tf_op jit(solution)/shard_map/ppermute | solution.py:35
  89.3 12.7 %collective-permute-start.16 = (bf16[4,8,32,256]{3,2,1,0:T(8,128)(2,1)S(1)}, bf16[4,8,32,256]{3,2,1,0:T(8,128)(2,1)}, u32[]{:S(2)}, u32[]{:S(2)}) collective-permute-start(bf16[4,8,32,256]{3,2,1,0:T(8,128)(2,1)S(1)} %pad_maximum_fusion.1.refs_14_), channel_id=1, source_target_pairs={{0,24},{8,0},{16,8},{24,16},{1,25},{9,1},{17,9},{25,17},{2,26},{10... | collective-permute-start | bytes 1572872 | tf_op jit(solution)/shard_map/ppermute | solution.py:35
  91.8 17.8 %collective-permute-start.21 = (bf16[4,8,32,256]{3,2,1,0:T(8,128)(2,1)S(1)}, bf16[4,8,32,256]{3,2,1,0:T(8,128)(2,1)S(1)}, u32[]{:S(2)}, u32[]{:S(2)}) collective-permute-start(bf16[4,8,32,256]{3,2,1,0:T(8,128)(2,1)S(1)} %pad_maximum_fusion.refs_4_), channel_id=1, source_target_pairs={{0,4},{4,0},{1,5},{5,1},{2,6},{6,2},{3,7},{7,3},{8,12},{12,8},{9,1... | collective-permute-start | bytes 1572872 | tf_op jit(solution)/shard_map/ppermute | solution.py:35
  102.0 11.6 %collective-permute-start.17 = (bf16[2,8,32,256]{3,2,1,0:T(8,128)(2,1)S(1)}, bf16[2,8,32,256]{3,2,1,0:T(8,128)(2,1)S(1)}, u32[]{:S(2)}, u32[]{:S(2)}) collective-permute-start(bf16[2,8,32,256]{3,2,1,0:T(8,128)(2,1)S(1)} %slice.50), channel_id=1, source_target_pairs={{0,1},{1,2},{2,3},{3,0},{4,5},{5,6},{6,7},{7,4},{8,9},{9,10},{10,1... | collective-permute-start | bytes 786440 | tf_op jit(solution)/shard_map/ppermute | solution.py:35
  102.1 11.6 %collective-permute-start.18 = (bf16[2,8,32,256]{3,2,1,0:T(8,128)(2,1)S(1)}, bf16[2,8,32,256]{3,2,1,0:T(8,128)(2,1)S(1)}, u32[]{:S(2)}, u32[]{:S(2)}) collective-permute-start(bf16[2,8,32,256]{3,2,1,0:T(8,128)(2,1)S(1)} %slice.51), channel_id=1, source_target_pairs={{0,3},{1,0},{2,1},{3,2},{4,7},{5,4},{6,5},{7,6},{8,11},{9,8},{10,9... | collective-permute-start | bytes 786440 | tf_op jit(solution)/shard_map/ppermute | solution.py:35
  105.9 8.3 %collective-permute-start.19 = (bf16[2,8,32,256]{3,2,1,0:T(8,128)(2,1)S(1)}, bf16[2,8,32,256]{3,2,1,0:T(8,128)(2,1)S(1)}, u32[]{:S(2)}, u32[]{:S(2)}) collective-permute-start(bf16[2,8,32,256]{3,2,1,0:T(8,128)(2,1)S(1)} %slice.52), channel_id=1, source_target_pairs={{0,8},{8,16},{16,24},{24,0},{1,9},{9,17},{17,25},{25,1},{2,10},{10... | collective-permute-start | bytes 786440 | tf_op jit(solution)/shard_map/ppermute | solution.py:35
  106.9 10.0 %collective-permute-start.20 = (bf16[2,8,32,256]{3,2,1,0:T(8,128)(2,1)S(1)}, bf16[2,8,32,256]{3,2,1,0:T(8,128)(2,1)S(1)}, u32[]{:S(2)}, u32[]{:S(2)}) collective-permute-start(bf16[2,8,32,256]{3,2,1,0:T(8,128)(2,1)S(1)} %slice.53), channel_id=1, source_target_pairs={{0,24},{8,0},{16,8},{24,16},{1,25},{9,1},{17,9},{25,17},{2,26},{10... | collective-permute-start | bytes 786440 | tf_op jit(solution)/shard_map/ppermute | solution.py:35
  109.7 10.0 %collective-permute-start.26 = (bf16[4,8,32,256]{3,2,1,0:T(8,128)(2,1)S(1)}, bf16[4,8,32,256]{3,2,1,0:T(8,128)(2,1)}, u32[]{:S(2)}, u32[]{:S(2)}) collective-permute-start(bf16[4,8,32,256]{3,2,1,0:T(8,128)(2,1)S(1)} %pad_maximum_fusion.1.refs_14_), channel_id=1, source_target_pairs={{0,4},{4,0},{1,5},{5,1},{2,6},{6,2},{3,7},{7,3},{8,12},{12,8},{9,1... | collective-permute-start | bytes 1572872 | tf_op jit(solution)/shard_map/ppermute | solution.py:35
  113.6 6.0 %collective-permute-start.22 = (bf16[4,8,32,256]{3,2,1,0:T(8,128)(2,1)S(1)}, bf16[4,8,32,256]{3,2,1,0:T(8,128)(2,1)}, u32[]{:S(2)}, u32[]{:S(2)}) collective-permute-start(bf16[4,8,32,256]{3,2,1,0:T(8,128)(2,1)S(1)} %collective-permute-done.13.refs_6_), channel_id=1, source_target_pairs={{0,4},{4,0},{1,5},{5,1},{2,6},{6,2},{3,7},{7,3},{8,12},{12,8},{9,1... | collective-permute-start | bytes 1572872 | tf_op jit(solution)/shard_map/ppermute | solution.py:35
  113.7 6.4 %collective-permute-start.23 = (bf16[4,8,32,256]{3,2,1,0:T(8,128)(2,1)S(1)}, bf16[4,8,32,256]{3,2,1,0:T(8,128)(2,1)}, u32[]{:S(2)}, u32[]{:S(2)}) collective-permute-start(bf16[4,8,32,256]{3,2,1,0:T(8,128)(2,1)S(1)} %collective-permute-done.14.refs_8_), channel_id=1, source_target_pairs={{0,4},{4,0},{1,5},{5,1},{2,6},{6,2},{3,7},{7,3},{8,12},{12,8},{9,1... | collective-permute-start | bytes 1572872 | tf_op jit(solution)/shard_map/ppermute | solution.py:35
  114.1 6.1 %collective-permute-start.27 = (bf16[4,8,32,256]{3,2,1,0:T(8,128)(2,1)}, bf16[4,8,32,256]{3,2,1,0:T(8,128)(2,1)}, u32[]{:S(2)}, u32[]{:S(2)}) collective-permute-start(bf16[4,8,32,256]{3,2,1,0:T(8,128)(2,1)} %collective-permute-done.15.refs_16_), channel_id=1, source_target_pairs={{0,4},{4,0},{1,5},{5,1},{2,6},{6,2},{3,7},{7,3},{8,12},{12,8},{9,1... | collective-permute-start | bytes 1572872 | tf_op jit(solution)/shard_map/ppermute | solution.py:35
  117.6 3.6 %collective-permute-start.28 = (bf16[4,8,32,256]{3,2,1,0:T(8,128)(2,1)}, bf16[4,8,32,256]{3,2,1,0:T(8,128)(2,1)}, u32[]{:S(2)}, u32[]{:S(2)}) collective-permute-start(bf16[4,8,32,256]{3,2,1,0:T(8,128)(2,1)} %collective-permute-done.16.refs_18_), channel_id=1, source_target_pairs={{0,4},{4,0},{1,5},{5,1},{2,6},{6,2},{3,7},{7,3},{8,12},{12,8},{9,1... | collective-permute-start | bytes 1572872 | tf_op jit(solution)/shard_map/ppermute | solution.py:35
  145.7 16.5 %all-to-all-start.4 = ((bf16[4,208,512]{2,1,0:T(8,128)(2,1)}), bf16[4,208,512]{2,1,0:T(8,128)(2,1)S(1)}, u32[]{:S(2)}, u32[]{:S(2)}) async-start(bf16[4,208,512]{2,1,0:T(8,128)(2,1)} %shard_map.148), calls=%async_computation.4 | async-start | bytes 1703936 | tf_op jit(solution)/shard_map/all_to_all | solution.py:29
  (24 other events, 206.9 us)
where the time goes:
time: 166 us; the launch traced here: 165 us
  starting transfers between devices  64.3 us (39%)
  waiting for transfers between devices  52 us (31%)
  Pallas kernels  27.5 us (17%)
  local copies, waits for them, and re-layouts  8.1 us (5%)
  matrix products  6.36 us (4%)
  other arithmetic  4.88 us (3%)
  between operations  1.69 us (1%)
    ppermute x31, starting transfers between devices, shift(): return lax.ppermute(v, axis, [(i, (i + k) % n) for i in range(n)])  39 us
    all_to_all x5, waiting for transfers between devices, exchange(): return lax.all_to_all(v, axis, 0, 0, tiled=True)  26.4 us
    ppermute x31, waiting for transfers between devices, shift(): return lax.ppermute(v, axis, [(i, (i + k) % n) for i in range(n)])  25.6 us
    all_to_all x5, starting transfers between devices, exchange(): return lax.all_to_all(v, axis, 0, 0, tiled=True)  25.3 us
    pallas_call x1, Pallas kernels, decode(): pl.pallas_call(functools.partial(decode_kernel, width), in_specs=[pl.Bloc...  22.5 us
    pallas_call x2, Pallas kernels, core_rows(): pl.pallas_call(functools.partial(core_rows_kernel, bool(got)), in_specs=[...  5.04 us
  transfers between devices with their start and end apart: 36, of which 16 were waited for; matrix products, arithmetic and copies ran while one was open for 8% of the time, Pallas kernels for 0%

commit v1 on v0

--- a/solution.py
+++ b/solution.py
@@ -80,20 +80,35 @@
             pltpu.SemaphoreType.DMA((nx,)),
             pltpu.SemaphoreType.DMA((nx,)),
         ],
-        compiler_params=pltpu.CompilerParams(vmem_limit_bytes=VMEM_LIMIT),
+        compiler_params=pltpu.CompilerParams(vmem_limit_bytes=57 * 2**20),
     )(core[None].astype(jnp.int32), g, *got)
 
 
-def decode_kernel(width, place, slots_ref, envs_ref, table_ref, gain_ref, *refs):
+def decode_kernel(width, place, slots_ref, envs_ref, table_from, gain_ref, *refs):
     n_pieces = 2 * len(PARTS) * NC
-    heads, refs = refs[:NY], refs[NY:]
-    pieces, (out_ref, w_ref, hidden, mixed, state, sems) = refs[:n_pieces], refs[n_pieces:]
+    heads_from, refs = refs[:NY], refs[NY:]
+    pieces, refs = refs[:n_pieces], refs[n_pieces:]
+    out_ref, w_ref, hidden, mixed, state, tags_ref, table_ref, heads, sems, row_sems = refs
     my_x, my_c, my_y = place[0], place[1], place[2]
     blocks, wide = w_ref.shape[0], w_ref.shape[-1]
     slots, own = slots_ref.shape[0], envs_ref.shape[0]
     m = slots + own
     tail = out_ref.shape[1] - slots
-    copies = ([], [])
+    early = [
+        (slots_ref.at[:, :width], state.at[:slots]),
+        (envs_ref.at[:, :width], state.at[slots:]),
+        (slots_ref.at[:, width:], tags_ref.at[:slots]),
+        (envs_ref.at[:, width:], tags_ref.at[slots:]),
+        (table_from, table_ref),
+    ]
+    late = [(heads_from[k], heads.at[k]) for k in range(NY)]
+    early, late = (
+        [pltpu.make_async_copy(a, b, row_sems.at[base + i]) for i, (a, b) in enumerate(group)]
+        for group, base in ((early, 0), (late, len(early)))
+    )
+    for copy in early:
+        copy.start()
+    copies = []
     for p in range(n_pieces):
         second, rest = divmod(p, len(PARTS) * NC)
         (k, begin, count), other = PARTS[rest // NC], rest % NC
@@ -108,15 +123,14 @@
                 sems.at[((second * NX + k) * NX + i) * NC + other],
             )
             copy.start()
-            copies[second].append(copy)
+            copies.append(copy)
 
     actions = table_ref.shape[0]
     number = lax.broadcasted_iota(jnp.int32, (m, actions), 1) + 1
     lanes = 128
 
     def onehot(step):
-        tags = [ref[:, width:].astype(F32) for ref in (slots_ref, envs_ref)]
-        tags = jnp.concatenate(tags, 0)
+        tags = tags_ref[...].astype(F32)
         chosen = lax.broadcasted_iota(jnp.int32, tags.shape, 1) == step
         tag = jnp.sum(jnp.where(chosen, tags, 0.0), axis=1, keepdims=True).astype(jnp.int32)
         return jnp.where(tag == number, 1.0, 0.0).astype(BF16)
@@ -125,13 +139,15 @@
         embedded = jnp.dot(hot, table_ref[:, cols], preferred_element_type=F32)
         hidden[:, cols] = (old.astype(F32) + embedded).astype(BF16)
 
+    for copy in late:
+        copy.start()
+    for copy in early:
+        copy.wait()
     hot = onehot(0)
     for n in range(blocks):
         cols = slice(n * wide, (n + 1) * wide)
-        state[:slots, cols] = slots_ref[:, cols]
-        state[slots:, cols] = envs_ref[:, cols]
         embed(hot, cols, state[:, cols])
-    for copy in copies[0] + copies[1]:
+    for copy in copies + late:
         copy.wait()
 
     def control_step(step, carry):
@@ -160,14 +176,14 @@
         out_ref[y, :slots, :] = state[:slots, 2 * y * wide : 2 * (y + 1) * wide]
     for k in range(NY):
         scores = lax.dot_general(
+            heads[k],
             state[slots:m, :],
-            heads[k][...],
             (((1,), (1,)), ((), ())),
             preferred_element_type=F32,
         )
-        row = my_y * own + lax.broadcasted_iota(jnp.int32, scores.shape, 0)
+        row = my_y * own + lax.broadcasted_iota(jnp.int32, scores.shape, 1)
         scores = (scores * jnp.where(row < place[3], 1.0, 0.0)).astype(BF16)
-        packed = [scores[i * tail : (i + 1) * tail] for i in range(own // tail)]
+        packed = [scores[i * tail : (i + 1) * tail] for i in range(scores.shape[0] // tail)]
         out_ref[lax.rem(my_y + k, NY), slots:, :] = jnp.concatenate(packed, 1)
 
 
@@ -175,12 +191,13 @@
     slots, own, width = slot_rows.shape[0], env_rows.shape[0], table.shape[1]
     wide, m = width // NY // 2, slots + own
     tail = own * heads[0].shape[0] // (width // NY)
-    vmem = pl.BlockSpec(memory_space=pltpu.VMEM)
+    vmem, hbm = pl.BlockSpec(memory_space=pltpu.VMEM), pl.BlockSpec(memory_space=pl.ANY)
     return pl.pallas_call(
         functools.partial(decode_kernel, width),
         in_specs=[pl.BlockSpec(memory_space=pltpu.SMEM)]
-        + [vmem] * (4 + NY)
-        + [pl.BlockSpec(memory_space=pl.ANY)] * len(pieces),
+        + [hbm] * 3
+        + [vmem]
+        + [hbm] * (NY + len(pieces)),
         out_specs=vmem,
         out_shape=jax.ShapeDtypeStruct((NY, slots + tail, width // NY), BF16),
         scratch_shapes=[
@@ -188,7 +205,11 @@
             pltpu.VMEM((m, width), BF16),
             pltpu.VMEM((m, width), BF16),
             pltpu.VMEM((m, width), BF16),
+            pltpu.VMEM((m, TAGS), BF16),
+            pltpu.VMEM(table.shape, BF16),
+            pltpu.VMEM((NY, *heads[0].shape), BF16),
             pltpu.SemaphoreType.DMA((2 * NX * NX * NC,)),
+            pltpu.SemaphoreType.DMA((5 + NY,)),
         ],
         compiler_params=pltpu.CompilerParams(vmem_limit_bytes=VMEM_LIMIT),
         cost_estimate=pl.CostEstimate(
@@ -224,7 +245,7 @@
 
     g = grad_parts[0].reshape(NZ, NX, NC, rows, cols)
     both = core_rows(my_c, g, swap(core_rows(1 - my_c, g)))
-    both, head = lax.optimization_barrier((both, head))
+    both, head, place = lax.optimization_barrier((both, head, place))
     by_x = exchange(both, "x")
     head = head.T
     heads = [head, shift(head, "y", 3, NY), None, shift(head, "y", 1, NY)]
@@ -294,14 +315,14 @@
     landed = exchange(final, "y")
 
     each = head.shape[0]
-    scores = landed[:, slots:].astype(F32).reshape(NY, -1, cols // each, each)
-    logits = jnp.transpose(scores, (0, 2, 1, 3)).reshape(env_slots, each)
+    scores = landed[:, slots:].astype(F32).reshape(NY, -1, cols // own, own)
+    logits = jnp.transpose(scores, (2, 1, 0, 3)).reshape(each, env_slots).T
 
     row = jnp.arange(owner_num * capacity, dtype=jnp.int32)
-    at = row % capacity // share * slots + row // capacity * share + row % share
-    order = (at[:, None] == row[None, :]).astype(BF16)
-    landed = landed[:, :slots].reshape(owner_num * capacity, cols)
-    received = jnp.dot(order, landed, preferred_element_type=F32)
+    deep = landed.shape[1]
+    at = row % capacity // share * deep + row // capacity * share + row % share
+    order = (at[:, None] == jnp.arange(NY * deep, dtype=jnp.int32)[None, :]).astype(BF16)
+    received = jnp.dot(order, landed.reshape(NY * deep, cols), preferred_element_type=F32)
     return (m_new, v_new, w_new, logits, received.astype(BF16))
 
 

time: 166 us -> 166 us (level)
  no operation moved by 1% of the time
where the time goes in v1:
time: 166 us; the launch traced here: 165 us
  starting transfers between devices  63.4 us (38%)
  waiting for transfers between devices  53.2 us (32%)
  Pallas kernels  27.7 us (17%)
  local copies, waits for them, and re-layouts  7.92 us (5%)
  matrix products  6.56 us (4%)
  other arithmetic  4.89 us (3%)
  between operations  1.68 us (1%)
    ppermute x31, starting transfers between devices, shift(): return lax.ppermute(v, axis, [(i, (i + k) % n) for i in range(n)])  38.6 us
    all_to_all x5, waiting for transfers between devices, exchange(): return lax.all_to_all(v, axis, 0, 0, tiled=True)  26.7 us
    ppermute x31, waiting for transfers between devices, shift(): return lax.ppermute(v, axis, [(i, (i + k) % n) for i in range(n)])  26.5 us
    all_to_all x5, starting transfers between devices, exchange(): return lax.all_to_all(v, axis, 0, 0, tiled=True)  24.8 us
    pallas_call x1, Pallas kernels, decode(): pl.pallas_call(functools.partial(decode_kernel, width), in_specs=[pl.Bloc...  22.7 us
    pallas_call x2, Pallas kernels, core_rows(): pl.pallas_call(functools.partial(core_rows_kernel, bool(got)), in_specs=[...  5.04 us
  transfers between devices with their start and end apart: 36, of which 16 were waited for; matrix products, arithmetic and copies ran while one was open for 8% of the time, Pallas kernels for 0%

profile of v1, /device:TPU:1, one launch (start us, length us, event | category | flops | bytes accessed | tf_op | source)
XLA Modules:
  0.0 165.4 jit_solution(7153309065159601057)
XLA Ops:
  0.6 2.4 %shard_map.146 = bf16[4,8,32,512]{3,2,1,0:T(8,128)(2,1)} custom-call(s32[1]{0:T(128)} %bitcast.2.core, f32[8,4,2,32,512]{4,3,2,1,0:T(8,128)} %bitcast.56), custom_call_target="tpu_custom_call" | custom-call | tf_op jit(solution)/shard_map/pallas_call | solution.py:70
  3.0 3.3 %collective-permute-start = (bf16[4,8,32,512]{3,2,1,0:T(8,128)(2,1)}, bf16[4,8,32,512]{3,2,1,0:T(8,128)(2,1)S(1)}, u32[]{:S(2)}, u32[]{:S(2)}) collective-permute-start(bf16[4,8,32,512]{3,2,1,0:T(8,128)(2,1)} %shard_map.146), channel_id=1, source_target_pairs={{0,4},{4,0},{1,5},{5,1},{2,6},{6,2},{3,7},{7,3},{8,12},{12,8},{9,1... | collective-permute-start | bytes 3145736 | tf_op jit(solution)/shard_map/ppermute | solution.py:35
  10.1 2.7 %shard_map.147 = bf16[4,8,32,512]{3,2,1,0:T(8,128)(2,1)} custom-call(s32[1]{0:T(128)} %bitcast.core, f32[8,4,2,32,512]{4,3,2,1,0:T(8,128)} %bitcast.57, bf16[4,8,32,512]{3,2,1,0:T(8,128)(2,1)} %copy-done.2), custom_call_target="tpu_custom_call" | custom-call | tf_op jit(solution)/shard_map/pallas_call | solution.py:70
  12.8 3.7 %all-to-all-start = ((bf16[4,8,32,512]{3,2,1,0:T(8,128)(2,1)}), bf16[4,8,32,512]{3,2,1,0:T(8,128)(2,1)S(1)}, u32[]{:S(2)}, u32[]{:S(2)}) async-start(bf16[4,8,32,512]{3,2,1,0:T(8,128)(2,1)} %shard_map.147), calls=%async_computation | async-start | bytes 2097152 | tf_op jit(solution)/shard_map/all_to_all | solution.py:29
  16.6 1.6 collective-permute-start.1
  18.4 6.4 %collective-permute-done.1.refs_1_ = bf16[64,2048]{1,0:T(8,128)(2,1)} collective-permute-done((bf16[64,2048]{1,0:T(8,128)(2,1)}, bf16[64,2048]{1,0:T(8,128)(2,1)}, u32[]{:S(2)}, u32[]{:S(2)}) %collective-permute-start.1) | collective-permute-done | bytes 262176 | tf_op jit(solution)/shard_map/ppermute | solution.py:35
  24.8 2.1 %collective-permute-done.2.refs_3_ = bf16[64,2048]{1,0:T(8,128)(2,1)} collective-permute-done((bf16[64,2048]{1,0:T(8,128)(2,1)}, bf16[64,2048]{1,0:T(8,128)(2,1)}, u32[]{:S(2)}, u32[]{:S(2)}) %collective-permute-start.2) | collective-permute-done | bytes 262176 | tf_op jit(solution)/shard_map/ppermute | solution.py:35
  26.8 4.7 %all-to-all-done = bf16[4,8,32,512]{3,2,1,0:T(8,128)(2,1)S(1)} async-done(((bf16[4,8,32,512]{3,2,1,0:T(8,128)(2,1)}), bf16[4,8,32,512]{3,2,1,0:T(8,128)(2,1)S(1)}, u32[]{:S(2)}, u32[]{:S(2)}) %all-to-all-start) | async-done | bytes 1048608 | tf_op jit(solution)/shard_map/all_to_all | solution.py:29
  32.4 6.7 %all-to-all-start.1 = ((bf16[8,32,512]{2,1,0:T(8,128)(2,1)}), bf16[8,32,512]{2,1,0:T(8,128)(2,1)S(1)}, u32[]{:S(2)}, u32[]{:S(2)}) async-start(bf16[8,32,512]{2,1,0:T(8,128)(2,1)} %reduce_sum.30), calls=%async_computation.1 | async-start | bytes 524288 | tf_op jit(solution)/shard_map/all_to_all | solution.py:29
  42.6 2.9 %collective-permute-start.6 = (bf16[64,2048]{1,0:T(8,128)(2,1)}, bf16[64,2048]{1,0:T(8,128)(2,1)}, u32[]{:S(2)}, u32[]{:S(2)}) collective-permute-start(bf16[64,2048]{1,0:T(8,128)(2,1)} %bitcast.5.refs_0_), channel_id=1, source_target_pairs={{0,2},{1,3},{2,0},{3,1},{4,6},{5,7},{6,4},{7,5},{8,10},{9,11},{10,... | collective-permute-start | bytes 786440 | tf_op jit(solution)/shard_map/ppermute | solution.py:35
  45.7 3.3 %all-to-all-done.1 = bf16[8,32,512]{2,1,0:T(8,128)(2,1)S(1)} async-done(((bf16[8,32,512]{2,1,0:T(8,128)(2,1)}), bf16[8,32,512]{2,1,0:T(8,128)(2,1)S(1)}, u32[]{:S(2)}, u32[]{:S(2)}) %all-to-all-start.1) | async-done | bytes 262176 | tf_op jit(solution)/shard_map/all_to_all | solution.py:29
  51.3 3.4 %all-to-all-start.2 = ((bf16[8,32,512]{2,1,0:T(8,128)(2,1)}), bf16[8,32,512]{2,1,0:T(8,128)(2,1)S(1)}, u32[]{:S(2)}, u32[]{:S(2)}) async-start(bf16[8,32,512]{2,1,0:T(8,128)(2,1)} %broadcast_in_dim.14), calls=%async_computation.2 | async-start | bytes 524288 | tf_op jit(solution)/shard_map/all_to_all | solution.py:29
  55.6 2.7 %convolution_convert_fusion = bf16[256,2176]{1,0:T(8,128)(2,1)} fusion(bf16[48,2176]{1,0:T(8,128)(2,1)} %collective-permute-done.5, bf16[48,2176]{1,0:T(8,128)(2,1)} %collective-permute-done.4, bf16[48,2176]{1,0:T(8,128)(2,1)} %collective-permute-done.3, bf16[48,2176]{1,0:T(8,128)(2,1)S(1)} %get-tuple-element.61, s32[256]{0:T(256)S(1)} %compare_select_fusion.4), kind=kOutput, calls=%fused_computation.2 | convolution fusion | flops 217858048 | bytes 1950720 | tf_op jit(solution)/shard_map/dot_general | solution.py:284
  58.2 5.8 %all-to-all-done.2 = bf16[8,32,512]{2,1,0:T(8,128)(2,1)S(1)} async-done(((bf16[8,32,512]{2,1,0:T(8,128)(2,1)}), bf16[8,32,512]{2,1,0:T(8,128)(2,1)S(1)}, u32[]{:S(2)}, u32[]{:S(2)}) %all-to-all-start.2) | async-done | bytes 262176 | tf_op jit(solution)/shard_map/all_to_all | solution.py:29
  64.0 7.5 %all-to-all-start.3 = ((bf16[16,16,2176]{2,1,0:T(8,128)(2,1)}), bf16[16,16,2176]{2,1,0:T(8,128)(2,1)S(1)}, u32[]{:S(2)}, u32[]{:S(2)}) async-start(bf16[16,16,2176]{2,1,0:T(8,128)(2,1)} %bitcast.10), calls=%async_computation.3 | async-start | bytes 2228224 | tf_op jit(solution)/shard_map/all_to_all | solution.py:29
  71.6 3.0 %collective-permute-start.9 = (bf16[8,32,256]{2,1,0:T(8,128)(2,1)S(1)}, bf16[8,32,256]{2,1,0:T(8,128)(2,1)S(1)}, u32[]{:S(2)}, u32[]{:S(2)}) collective-permute-start(bf16[8,32,256]{2,1,0:T(8,128)(2,1)S(1)} %get-tuple-element.68), channel_id=1, source_target_pairs={{0,24},{8,0},{16,8},{24,16},{1,25},{9,1},{17,9},{25,17},{2,26},{10... | collective-permute-start | bytes 393224 | tf_op jit(solution)/shard_map/ppermute | solution.py:35
  78.0 2.0 %collective-permute-done.9 = bf16[8,32,256]{2,1,0:T(8,128)(2,1)S(1)} collective-permute-done((bf16[8,32,256]{2,1,0:T(8,128)(2,1)S(1)}, bf16[8,32,256]{2,1,0:T(8,128)(2,1)S(1)}, u32[]{:S(2)}, u32[]{:S(2)}) %collective-permute-start.9) | collective-permute-done | bytes 131104 | tf_op jit(solution)/shard_map/ppermute | solution.py:35
  80.7 3.7 %collective-permute-done.7 = bf16[8,32,256]{2,1,0:T(8,128)(2,1)S(1)} collective-permute-done((bf16[8,32,256]{2,1,0:T(8,128)(2,1)S(1)}, bf16[8,32,256]{2,1,0:T(8,128)(2,1)S(1)}, u32[]{:S(2)}, u32[]{:S(2)}) %collective-permute-start.7) | collective-permute-done | bytes 131104 | tf_op jit(solution)/shard_map/ppermute | solution.py:35
  84.5 2.1 %collective-permute-done.10 = bf16[8,32,256]{2,1,0:T(8,128)(2,1)S(1)} collective-permute-done((bf16[8,32,256]{2,1,0:T(8,128)(2,1)S(1)}, bf16[8,32,256]{2,1,0:T(8,128)(2,1)S(1)}, u32[]{:S(2)}, u32[]{:S(2)}) %collective-permute-start.10) | collective-permute-done | bytes 131104 | tf_op jit(solution)/shard_map/ppermute | solution.py:35
  86.7 2.7 %collective-permute-start.14 = (bf16[4,8,32,256]{3,2,1,0:T(8,128)(2,1)S(1)}, bf16[4,8,32,256]{3,2,1,0:T(8,128)(2,1)S(1)}, u32[]{:S(2)}, u32[]{:S(2)}) collective-permute-start(bf16[4,8,32,256]{3,2,1,0:T(8,128)(2,1)S(1)} %pad_maximum_fusion.refs_4_), channel_id=1, source_target_pairs={{0,3},{1,0},{2,1},{3,2},{4,7},{5,4},{6,5},{7,6},{8,11},{9,8},{10,9... | collective-permute-start | bytes 1572872 | tf_op jit(solution)/shard_map/ppermute | solution.py:35
  89.5 2.5 %collective-permute-start.16 = (bf16[4,8,32,256]{3,2,1,0:T(8,128)(2,1)S(1)}, bf16[4,8,32,256]{3,2,1,0:T(8,128)(2,1)}, u32[]{:S(2)}, u32[]{:S(2)}) collective-permute-start(bf16[4,8,32,256]{3,2,1,0:T(8,128)(2,1)S(1)} %pad_maximum_fusion.1.refs_14_), channel_id=1, source_target_pairs={{0,24},{8,0},{16,8},{24,16},{1,25},{9,1},{17,9},{25,17},{2,26},{10... | collective-permute-start | bytes 1572872 | tf_op jit(solution)/shard_map/ppermute | solution.py:35
  92.1 2.4 %collective-permute-start.21 = (bf16[4,8,32,256]{3,2,1,0:T(8,128)(2,1)S(1)}, bf16[4,8,32,256]{3,2,1,0:T(8,128)(2,1)S(1)}, u32[]{:S(2)}, u32[]{:S(2)}) collective-permute-start(bf16[4,8,32,256]{3,2,1,0:T(8,128)(2,1)S(1)} %pad_maximum_fusion.refs_4_), channel_id=1, source_target_pairs={{0,4},{4,0},{1,5},{5,1},{2,6},{6,2},{3,7},{7,3},{8,12},{12,8},{9,1... | collective-permute-start | bytes 1572872 | tf_op jit(solution)/shard_map/ppermute | solution.py:35
  94.5 5.6 %collective-permute-done.13.refs_6_ = bf16[4,8,32,256]{3,2,1,0:T(8,128)(2,1)S(1)} collective-permute-done((bf16[4,8,32,256]{3,2,1,0:T(8,128)(2,1)S(1)}, bf16[4,8,32,256]{3,2,1,0:T(8,128)(2,1)S(1)}, u32[]{:S(2)}, u32[]{:S(2)}) %collective-permute-start.13) | collective-permute-done | bytes 524320 | tf_op jit(solution)/shard_map/ppermute | solution.py:35
  100.2 2.1 %collective-permute-done.15.refs_16_ = bf16[4,8,32,256]{3,2,1,0:T(8,128)(2,1)} collective-permute-done((bf16[4,8,32,256]{3,2,1,0:T(8,128)(2,1)S(1)}, bf16[4,8,32,256]{3,2,1,0:T(8,128)(2,1)}, u32[]{:S(2)}, u32[]{:S(2)}) %collective-permute-start.15) | collective-permute-done | bytes 524320 | tf_op jit(solution)/shard_map/ppermute | solution.py:35
  102.4 2.7 %collective-permute-start.18 = (bf16[2,8,32,256]{3,2,1,0:T(8,128)(2,1)S(1)}, bf16[2,8,32,256]{3,2,1,0:T(8,128)(2,1)S(1)}, u32[]{:S(2)}, u32[]{:S(2)}) collective-permute-start(bf16[2,8,32,256]{3,2,1,0:T(8,128)(2,1)S(1)} %slice.48), channel_id=1, source_target_pairs={{0,3},{1,0},{2,1},{3,2},{4,7},{5,4},{6,5},{7,6},{8,11},{9,8},{10,9... | collective-permute-start | bytes 786440 | tf_op jit(solution)/shard_map/ppermute | solution.py:35
  107.3 2.6 %collective-permute-start.20 = (bf16[2,8,32,256]{3,2,1,0:T(8,128)(2,1)S(1)}, bf16[2,8,32,256]{3,2,1,0:T(8,128)(2,1)S(1)}, u32[]{:S(2)}, u32[]{:S(2)}) collective-permute-start(bf16[2,8,32,256]{3,2,1,0:T(8,128)(2,1)S(1)} %slice.50), channel_id=1, source_target_pairs={{0,24},{8,0},{16,8},{24,16},{1,25},{9,1},{17,9},{25,17},{2,26},{10... | collective-permute-start | bytes 786440 | tf_op jit(solution)/shard_map/ppermute | solution.py:35
  109.9 3.9 %collective-permute-start.26 = (bf16[4,8,32,256]{3,2,1,0:T(8,128)(2,1)S(1)}, bf16[4,8,32,256]{3,2,1,0:T(8,128)(2,1)}, u32[]{:S(2)}, u32[]{:S(2)}) collective-permute-start(bf16[4,8,32,256]{3,2,1,0:T(8,128)(2,1)S(1)} %pad_maximum_fusion.1.refs_14_), channel_id=1, source_target_pairs={{0,4},{4,0},{1,5},{5,1},{2,6},{6,2},{3,7},{7,3},{8,12},{12,8},{9,1... | collective-permute-start | bytes 1572872 | tf_op jit(solution)/shard_map/ppermute | solution.py:35
  114.4 2.8 %collective-permute-start.27 = (bf16[4,8,32,256]{3,2,1,0:T(8,128)(2,1)}, bf16[4,8,32,256]{3,2,1,0:T(8,128)(2,1)}, u32[]{:S(2)}, u32[]{:S(2)}) collective-permute-start(bf16[4,8,32,256]{3,2,1,0:T(8,128)(2,1)} %collective-permute-done.15.refs_16_), channel_id=1, source_target_pairs={{0,4},{4,0},{1,5},{5,1},{2,6},{6,2},{3,7},{7,3},{8,12},{12,8},{9,1... | collective-permute-start | bytes 1572872 | tf_op jit(solution)/shard_map/ppermute | solution.py:35
  123.5 22.7 %shard_map.148 = bf16[4,208,512]{2,1,0:T(8,128)(2,1)} custom-call(s32[4]{0:T(128)} %pad_add_fusion.place, bf16[192,2176]{1,0:T(8,128)(2,1)} %convolution_convert_fusion.1.slots_ref, bf16[128,2176]{1,0:T(8,128)(2,1)} %constant_dynamic-slice_fusion.envs_ref, bf16[256,2048]{1,0:T(8,128)(2,1)} %table_from.1, f32[1,2048]{1,0:T(1,128)} %bitcast.72, ...), custom_call_target="tpu_custom_call" | custom-call | flops 10737418240 | bytes 8388608 | tf_op jit(solution)/shard_map/pallas_call | solution.py:195
  146.2 3.5 %all-to-all-start.4 = ((bf16[4,208,512]{2,1,0:T(8,128)(2,1)}), bf16[4,208,512]{2,1,0:T(8,128)(2,1)S(1)}, u32[]{:S(2)}, u32[]{:S(2)}) async-start(bf16[4,208,512]{2,1,0:T(8,128)(2,1)} %shard_map.148), calls=%async_computation.4 | async-start | bytes 1703936 | tf_op jit(solution)/shard_map/all_to_all | solution.py:29
  149.7 12.9 %all-to-all-done.4 = bf16[4,208,512]{2,1,0:T(8,128)(2,1)S(1)} async-done(((bf16[4,208,512]{2,1,0:T(8,128)(2,1)}), bf16[4,208,512]{2,1,0:T(8,128)(2,1)S(1)}, u32[]{:S(2)}, u32[]{:S(2)}) %all-to-all-start.4) | async-done | bytes 852000 | tf_op jit(solution)/shard_map/all_to_all | solution.py:29
  163.5 1.9 %fusion.3 = bf16[768,512]{1,0:T(8,128)(2,1)} fusion(bf16[832,512]{1,0:T(8,128)(2,1)S(1)} %bitcast.59, s32[768]{0:T(1024)S(1)} %fusion.34), kind=kOutput, calls=%fused_computation.8 | convolution fusion | flops 655343616 | bytes 1641472 | tf_op jit(solution)/shard_map/dot_general | solution.py:325
  (120 shorter events, 25.5 us)
Async XLA Ops:
  3.0 6.1 %collective-permute-start = (bf16[4,8,32,512]{3,2,1,0:T(8,128)(2,1)}, bf16[4,8,32,512]{3,2,1,0:T(8,128)(2,1)S(1)}, u32[]{:S(2)}, u32[]{:S(2)}) collective-permute-start(bf16[4,8,32,512]{3,2,1,0:T(8,128)(2,1)} %shard_map.146), channel_id=1, source_target_pairs={{0,4},{4,0},{1,5},{5,1},{2,6},{6,2},{3,7},{7,3},{8,12},{12,8},{9,1... | collective-permute-start | bytes 3145736 | tf_op jit(solution)/shard_map/ppermute | solution.py:35
  12.8 18.7 %all-to-all-start = ((bf16[4,8,32,512]{3,2,1,0:T(8,128)(2,1)}), bf16[4,8,32,512]{3,2,1,0:T(8,128)(2,1)S(1)}, u32[]{:S(2)}, u32[]{:S(2)}) async-start(bf16[4,8,32,512]{3,2,1,0:T(8,128)(2,1)} %shard_map.147), calls=%async_computation | async-start | bytes 2097152 | tf_op jit(solution)/shard_map/all_to_all | solution.py:29
  16.6 8.2 %collective-permute-start.1 = (bf16[64,2048]{1,0:T(8,128)(2,1)}, bf16[64,2048]{1,0:T(8,128)(2,1)}, u32[]{:S(2)}, u32[]{:S(2)}) collective-permute-start(bf16[64,2048]{1,0:T(8,128)(2,1)} %bitcast.5.refs_0_), channel_id=1, source_target_pairs={{0,3},{1,0},{2,1},{3,2},{4,7},{5,4},{6,5},{7,6},{8,11},{9,8},{10,9... | collective-permute-start | bytes 786440 | tf_op jit(solution)/shard_map/ppermute | solution.py:35
  18.2 8.7 %collective-permute-start.2 = (bf16[64,2048]{1,0:T(8,128)(2,1)}, bf16[64,2048]{1,0:T(8,128)(2,1)}, u32[]{:S(2)}, u32[]{:S(2)}) collective-permute-start(bf16[64,2048]{1,0:T(8,128)(2,1)} %bitcast.5.refs_0_), channel_id=1, source_target_pairs={{0,1},{1,2},{2,3},{3,0},{4,5},{5,6},{6,7},{7,4},{8,9},{9,10},{10,1... | collective-permute-start | bytes 786440 | tf_op jit(solution)/shard_map/ppermute | solution.py:35
  32.4 16.5 %all-to-all-start.1 = ((bf16[8,32,512]{2,1,0:T(8,128)(2,1)}), bf16[8,32,512]{2,1,0:T(8,128)(2,1)S(1)}, u32[]{:S(2)}, u32[]{:S(2)}) async-start(bf16[8,32,512]{2,1,0:T(8,128)(2,1)} %reduce_sum.30), calls=%async_computation.1 | async-start | bytes 524288 | tf_op jit(solution)/shard_map/all_to_all | solution.py:29
  40.5 15.1 %collective-permute-start.5 = (bf16[48,2176]{1,0:T(8,128)(2,1)}, bf16[48,2176]{1,0:T(8,128)(2,1)}, u32[]{:S(2)}, u32[]{:S(2)}) collective-permute-start(bf16[48,2176]{1,0:T(8,128)(2,1)} %get-tuple-element.62), channel_id=1, source_target_pairs={{0,24},{8,0},{16,8},{24,16},{1,25},{9,1},{17,9},{25,17},{2,26},{10... | collective-permute-start | bytes 626696 | tf_op jit(solution)/shard_map/ppermute | solution.py:35
  41.4 14.2 %collective-permute-start.4 = (bf16[48,2176]{1,0:T(8,128)(2,1)S(1)}, bf16[48,2176]{1,0:T(8,128)(2,1)}, u32[]{:S(2)}, u32[]{:S(2)}) collective-permute-start(bf16[48,2176]{1,0:T(8,128)(2,1)S(1)} %get-tuple-element.63), channel_id=1, source_target_pairs={{0,16},{8,24},{16,0},{24,8},{1,17},{9,25},{17,1},{25,9},{2,18},{10... | collective-permute-start | bytes 626696 | tf_op jit(solution)/shard_map/ppermute | solution.py:35
  42.6 13.0 %collective-permute-start.3 = (bf16[48,2176]{1,0:T(8,128)(2,1)S(1)}, bf16[48,2176]{1,0:T(8,128)(2,1)}, u32[]{:S(2)}, u32[]{:S(2)}) collective-permute-start(bf16[48,2176]{1,0:T(8,128)(2,1)S(1)} %get-tuple-element.64), channel_id=1, source_target_pairs={{0,8},{8,16},{16,24},{24,0},{1,9},{9,17},{17,25},{25,1},{2,10},{10... | collective-permute-start | bytes 626696 | tf_op jit(solution)/shard_map/ppermute | solution.py:35
  42.6 15.6 %collective-permute-start.6 = (bf16[64,2048]{1,0:T(8,128)(2,1)}, bf16[64,2048]{1,0:T(8,128)(2,1)}, u32[]{:S(2)}, u32[]{:S(2)}) collective-permute-start(bf16[64,2048]{1,0:T(8,128)(2,1)} %bitcast.5.refs_0_), channel_id=1, source_target_pairs={{0,2},{1,3},{2,0},{3,1},{4,6},{5,7},{6,4},{7,5},{8,10},{9,11},{10,... | collective-permute-start | bytes 786440 | tf_op jit(solution)/shard_map/ppermute | solution.py:35
  51.3 12.7 %all-to-all-start.2 = ((bf16[8,32,512]{2,1,0:T(8,128)(2,1)}), bf16[8,32,512]{2,1,0:T(8,128)(2,1)S(1)}, u32[]{:S(2)}, u32[]{:S(2)}) async-start(bf16[8,32,512]{2,1,0:T(8,128)(2,1)} %broadcast_in_dim.14), calls=%async_computation.2 | async-start | bytes 524288 | tf_op jit(solution)/shard_map/all_to_all | solution.py:29
  64.0 54.5 %all-to-all-start.3 = ((bf16[16,16,2176]{2,1,0:T(8,128)(2,1)}), bf16[16,16,2176]{2,1,0:T(8,128)(2,1)S(1)}, u32[]{:S(2)}, u32[]{:S(2)}) async-start(bf16[16,16,2176]{2,1,0:T(8,128)(2,1)} %bitcast.10), calls=%async_computation.3 | async-start | bytes 2228224 | tf_op jit(solution)/shard_map/all_to_all | solution.py:29
  71.6 8.4 %collective-permute-start.9 = (bf16[8,32,256]{2,1,0:T(8,128)(2,1)S(1)}, bf16[8,32,256]{2,1,0:T(8,128)(2,1)S(1)}, u32[]{:S(2)}, u32[]{:S(2)}) collective-permute-start(bf16[8,32,256]{2,1,0:T(8,128)(2,1)S(1)} %get-tuple-element.68), channel_id=1, source_target_pairs={{0,24},{8,0},{16,8},{24,16},{1,25},{9,1},{17,9},{25,17},{2,26},{10... | collective-permute-start | bytes 393224 | tf_op jit(solution)/shard_map/ppermute | solution.py:35
  74.6 6.1 %collective-permute-start.8 = (bf16[8,32,256]{2,1,0:T(8,128)(2,1)S(1)}, bf16[8,32,256]{2,1,0:T(8,128)(2,1)S(1)}, u32[]{:S(2)}, u32[]{:S(2)}) collective-permute-start(bf16[8,32,256]{2,1,0:T(8,128)(2,1)S(1)} %get-tuple-element.68), channel_id=1, source_target_pairs={{0,16},{8,24},{16,0},{24,8},{1,17},{9,25},{17,1},{25,9},{2,18},{10... | collective-permute-start | bytes 393224 | tf_op jit(solution)/shard_map/ppermute | solution.py:35
  75.2 9.2 %collective-permute-start.7 = (bf16[8,32,256]{2,1,0:T(8,128)(2,1)S(1)}, bf16[8,32,256]{2,1,0:T(8,128)(2,1)S(1)}, u32[]{:S(2)}, u32[]{:S(2)}) collective-permute-start(bf16[8,32,256]{2,1,0:T(8,128)(2,1)S(1)} %get-tuple-element.68), channel_id=1, source_target_pairs={{0,8},{8,16},{16,24},{24,0},{1,9},{9,17},{17,25},{25,1},{2,10},{10... | collective-permute-start | bytes 393224 | tf_op jit(solution)/shard_map/ppermute | solution.py:35
  75.8 8.7 %collective-permute-start.12 = (bf16[8,32,256]{2,1,0:T(8,128)(2,1)S(1)}, bf16[8,32,256]{2,1,0:T(8,128)(2,1)S(1)}, u32[]{:S(2)}, u32[]{:S(2)}) collective-permute-start(bf16[8,32,256]{2,1,0:T(8,128)(2,1)S(1)} %get-tuple-element.67), channel_id=1, source_target_pairs={{0,3},{1,0},{2,1},{3,2},{4,7},{5,4},{6,5},{7,6},{8,11},{9,8},{10,9... | collective-permute-start | bytes 393224 | tf_op jit(solution)/shard_map/ppermute | solution.py:35
  76.6 7.9 %collective-permute-start.11 = (bf16[8,32,256]{2,1,0:T(8,128)(2,1)S(1)}, bf16[8,32,256]{2,1,0:T(8,128)(2,1)S(1)}, u32[]{:S(2)}, u32[]{:S(2)}) collective-permute-start(bf16[8,32,256]{2,1,0:T(8,128)(2,1)S(1)} %get-tuple-element.67), channel_id=1, source_target_pairs={{0,2},{1,3},{2,0},{3,1},{4,6},{5,7},{6,4},{7,5},{8,10},{9,11},{10,... | collective-permute-start | bytes 393224 | tf_op jit(solution)/shard_map/ppermute | solution.py:35
  80.0 6.6 %collective-permute-start.10 = (bf16[8,32,256]{2,1,0:T(8,128)(2,1)S(1)}, bf16[8,32,256]{2,1,0:T(8,128)(2,1)S(1)}, u32[]{:S(2)}, u32[]{:S(2)}) collective-permute-start(bf16[8,32,256]{2,1,0:T(8,128)(2,1)S(1)} %get-tuple-element.67), channel_id=1, source_target_pairs={{0,1},{1,2},{2,3},{3,0},{4,5},{5,6},{6,7},{7,4},{8,9},{9,10},{10,1... | collective-permute-start | bytes 393224 | tf_op jit(solution)/shard_map/ppermute | solution.py:35
  86.7 13.5 %collective-permute-start.13 = (bf16[4,8,32,256]{3,2,1,0:T(8,128)(2,1)S(1)}, bf16[4,8,32,256]{3,2,1,0:T(8,128)(2,1)S(1)}, u32[]{:S(2)}, u32[]{:S(2)}) collective-permute-start(bf16[4,8,32,256]{3,2,1,0:T(8,128)(2,1)S(1)} %pad_maximum_fusion.refs_4_), channel_id=1, source_target_pairs={{0,1},{1,2},{2,3},{3,0},{4,5},{5,6},{6,7},{7,4},{8,9},{9,10},{10,1... | collective-permute-start | bytes 1572872 | tf_op jit(solution)/shard_map/ppermute | solution.py:35
  86.7 13.4 %collective-permute-start.14 = (bf16[4,8,32,256]{3,2,1,0:T(8,128)(2,1)S(1)}, bf16[4,8,32,256]{3,2,1,0:T(8,128)(2,1)S(1)}, u32[]{:S(2)}, u32[]{:S(2)}) collective-permute-start(bf16[4,8,32,256]{3,2,1,0:T(8,128)(2,1)S(1)} %pad_maximum_fusion.refs_4_), channel_id=1, source_target_pairs={{0,3},{1,0},{2,1},{3,2},{4,7},{5,4},{6,5},{7,6},{8,11},{9,8},{10,9... | collective-permute-start | bytes 1572872 | tf_op jit(solution)/shard_map/ppermute | solution.py:35
  89.4 12.9 %collective-permute-start.15 = (bf16[4,8,32,256]{3,2,1,0:T(8,128)(2,1)S(1)}, bf16[4,8,32,256]{3,2,1,0:T(8,128)(2,1)}, u32[]{:S(2)}, u32[]{:S(2)}) collective-permute-start(bf16[4,8,32,256]{3,2,1,0:T(8,128)(2,1)S(1)} %pad_maximum_fusion.1.refs_14_), channel_id=1, source_target_pairs={{0,8},{8,16},{16,24},{24,0},{1,9},{9,17},{17,25},{25,1},{2,10},{10... | collective-permute-start | bytes 1572872 | tf_op jit(solution)/shard_map/ppermute | solution.py:35
  89.5 12.7 %collective-permute-start.16 = (bf16[4,8,32,256]{3,2,1,0:T(8,128)(2,1)S(1)}, bf16[4,8,32,256]{3,2,1,0:T(8,128)(2,1)}, u32[]{:S(2)}, u32[]{:S(2)}) collective-permute-start(bf16[4,8,32,256]{3,2,1,0:T(8,128)(2,1)S(1)} %pad_maximum_fusion.1.refs_14_), channel_id=1, source_target_pairs={{0,24},{8,0},{16,8},{24,16},{1,25},{9,1},{17,9},{25,17},{2,26},{10... | collective-permute-start | bytes 1572872 | tf_op jit(solution)/shard_map/ppermute | solution.py:35
  92.1 17.8 %collective-permute-start.21 = (bf16[4,8,32,256]{3,2,1,0:T(8,128)(2,1)S(1)}, bf16[4,8,32,256]{3,2,1,0:T(8,128)(2,1)S(1)}, u32[]{:S(2)}, u32[]{:S(2)}) collective-permute-start(bf16[4,8,32,256]{3,2,1,0:T(8,128)(2,1)S(1)} %pad_maximum_fusion.refs_4_), channel_id=1, source_target_pairs={{0,4},{4,0},{1,5},{5,1},{2,6},{6,2},{3,7},{7,3},{8,12},{12,8},{9,1... | collective-permute-start | bytes 1572872 | tf_op jit(solution)/shard_map/ppermute | solution.py:35
  102.3 11.6 %collective-permute-start.17 = (bf16[2,8,32,256]{3,2,1,0:T(8,128)(2,1)S(1)}, bf16[2,8,32,256]{3,2,1,0:T(8,128)(2,1)S(1)}, u32[]{:S(2)}, u32[]{:S(2)}) collective-permute-start(bf16[2,8,32,256]{3,2,1,0:T(8,128)(2,1)S(1)} %slice.47), channel_id=1, source_target_pairs={{0,1},{1,2},{2,3},{3,0},{4,5},{5,6},{6,7},{7,4},{8,9},{9,10},{10,1... | collective-permute-start | bytes 786440 | tf_op jit(solution)/shard_map/ppermute | solution.py:35
  102.4 11.6 %collective-permute-start.18 = (bf16[2,8,32,256]{3,2,1,0:T(8,128)(2,1)S(1)}, bf16[2,8,32,256]{3,2,1,0:T(8,128)(2,1)S(1)}, u32[]{:S(2)}, u32[]{:S(2)}) collective-permute-start(bf16[2,8,32,256]{3,2,1,0:T(8,128)(2,1)S(1)} %slice.48), channel_id=1, source_target_pairs={{0,3},{1,0},{2,1},{3,2},{4,7},{5,4},{6,5},{7,6},{8,11},{9,8},{10,9... | collective-permute-start | bytes 786440 | tf_op jit(solution)/shard_map/ppermute | solution.py:35
  106.1 8.3 %collective-permute-start.19 = (bf16[2,8,32,256]{3,2,1,0:T(8,128)(2,1)S(1)}, bf16[2,8,32,256]{3,2,1,0:T(8,128)(2,1)S(1)}, u32[]{:S(2)}, u32[]{:S(2)}) collective-permute-start(bf16[2,8,32,256]{3,2,1,0:T(8,128)(2,1)S(1)} %slice.49), channel_id=1, source_target_pairs={{0,8},{8,16},{16,24},{24,0},{1,9},{9,17},{17,25},{25,1},{2,10},{10... | collective-permute-start | bytes 786440 | tf_op jit(solution)/shard_map/ppermute | solution.py:35
  107.3 9.9 %collective-permute-start.20 = (bf16[2,8,32,256]{3,2,1,0:T(8,128)(2,1)S(1)}, bf16[2,8,32,256]{3,2,1,0:T(8,128)(2,1)S(1)}, u32[]{:S(2)}, u32[]{:S(2)}) collective-permute-start(bf16[2,8,32,256]{3,2,1,0:T(8,128)(2,1)S(1)} %slice.50), channel_id=1, source_target_pairs={{0,24},{8,0},{16,8},{24,16},{1,25},{9,1},{17,9},{25,17},{2,26},{10... | collective-permute-start | bytes 786440 | tf_op jit(solution)/shard_map/ppermute | solution.py:35
  109.9 10.0 %collective-permute-start.26 = (bf16[4,8,32,256]{3,2,1,0:T(8,128)(2,1)S(1)}, bf16[4,8,32,256]{3,2,1,0:T(8,128)(2,1)}, u32[]{:S(2)}, u32[]{:S(2)}) collective-permute-start(bf16[4,8,32,256]{3,2,1,0:T(8,128)(2,1)S(1)} %pad_maximum_fusion.1.refs_14_), channel_id=1, source_target_pairs={{0,4},{4,0},{1,5},{5,1},{2,6},{6,2},{3,7},{7,3},{8,12},{12,8},{9,1... | collective-permute-start | bytes 1572872 | tf_op jit(solution)/shard_map/ppermute | solution.py:35
  113.8 6.1 %collective-permute-start.22 = (bf16[4,8,32,256]{3,2,1,0:T(8,128)(2,1)S(1)}, bf16[4,8,32,256]{3,2,1,0:T(8,128)(2,1)}, u32[]{:S(2)}, u32[]{:S(2)}) collective-permute-start(bf16[4,8,32,256]{3,2,1,0:T(8,128)(2,1)S(1)} %collective-permute-done.13.refs_6_), channel_id=1, source_target_pairs={{0,4},{4,0},{1,5},{5,1},{2,6},{6,2},{3,7},{7,3},{8,12},{12,8},{9,1... | collective-permute-start | bytes 1572872 | tf_op jit(solution)/shard_map/ppermute | solution.py:35
  114.0 6.5 %collective-permute-start.23 = (bf16[4,8,32,256]{3,2,1,0:T(8,128)(2,1)S(1)}, bf16[4,8,32,256]{3,2,1,0:T(8,128)(2,1)}, u32[]{:S(2)}, u32[]{:S(2)}) collective-permute-start(bf16[4,8,32,256]{3,2,1,0:T(8,128)(2,1)S(1)} %collective-permute-done.14.refs_8_), channel_id=1, source_target_pairs={{0,4},{4,0},{1,5},{5,1},{2,6},{6,2},{3,7},{7,3},{8,12},{12,8},{9,1... | collective-permute-start | bytes 1572872 | tf_op jit(solution)/shard_map/ppermute | solution.py:35
  114.4 6.2 %collective-permute-start.27 = (bf16[4,8,32,256]{3,2,1,0:T(8,128)(2,1)}, bf16[4,8,32,256]{3,2,1,0:T(8,128)(2,1)}, u32[]{:S(2)}, u32[]{:S(2)}) collective-permute-start(bf16[4,8,32,256]{3,2,1,0:T(8,128)(2,1)} %collective-permute-done.15.refs_16_), channel_id=1, source_target_pairs={{0,4},{4,0},{1,5},{5,1},{2,6},{6,2},{3,7},{7,3},{8,12},{12,8},{9,1... | collective-permute-start | bytes 1572872 | tf_op jit(solution)/shard_map/ppermute | solution.py:35
  117.9 3.1 %collective-permute-start.28 = (bf16[4,8,32,256]{3,2,1,0:T(8,128)(2,1)}, bf16[4,8,32,256]{3,2,1,0:T(8,128)(2,1)}, u32[]{:S(2)}, u32[]{:S(2)}) collective-permute-start(bf16[4,8,32,256]{3,2,1,0:T(8,128)(2,1)} %collective-permute-done.16.refs_18_), channel_id=1, source_target_pairs={{0,4},{4,0},{1,5},{5,1},{2,6},{6,2},{3,7},{7,3},{8,12},{12,8},{9,1... | collective-permute-start | bytes 1572872 | tf_op jit(solution)/shard_map/ppermute | solution.py:35
  146.2 16.5 %all-to-all-start.4 = ((bf16[4,208,512]{2,1,0:T(8,128)(2,1)}), bf16[4,208,512]{2,1,0:T(8,128)(2,1)S(1)}, u32[]{:S(2)}, u32[]{:S(2)}) async-start(bf16[4,208,512]{2,1,0:T(8,128)(2,1)} %shard_map.148), calls=%async_computation.4 | async-start | bytes 1703936 | tf_op jit(solution)/shard_map/all_to_all | solution.py:29
  (24 other events, 208.1 us)

commit v2 on v1

--- a/solution.py
+++ b/solution.py
@@ -150,7 +150,7 @@
     for copy in copies + late:
         copy.wait()
 
-    def control_step(step, carry):
+    def control_step(step, last):
         total = jnp.zeros((m, lanes), F32)
         for n in range(blocks):
             w = w_ref[n].reshape(width, wide)
@@ -161,19 +161,23 @@
                 total = total + got[:, at : at + lanes] * got[:, at : at + lanes]
         total = jnp.sum(total, axis=1, keepdims=True)
         inverse = lax.rsqrt(total * (1.0 / width) + norm_eps)
-        hot = onehot(step + 1)
+        hot = None if last else onehot(step + 1)
         for n in range(blocks):
             cols = slice(n * wide, (n + 1) * wide)
             old = state[:, cols].astype(F32)
             new = old + gain_ref[:, cols] * mixed[:, cols].astype(F32) * inverse
             new = new.astype(BF16)
-            state[:, cols] = new
-            embed(hot, cols, new)
-        return carry
-
-    lax.fori_loop(0, STEPS, control_step, 0)
-    for y in range(NY):
-        out_ref[y, :slots, :] = state[:slots, 2 * y * wide : 2 * (y + 1) * wide]
+            if last:
+                out_cols = slice(n % 2 * wide, (n % 2 + 1) * wide)
+                out_ref[n // 2, :slots, out_cols] = new[:slots]
+                state[slots:, cols] = new[slots:]
+            else:
+                state[:, cols] = new
+                embed(hot, cols, new)
+        return 0
+
+    lax.fori_loop(0, STEPS - 1, lambda step, _: control_step(step, False), 0)
+    control_step(STEPS - 1, True)
     for k in range(NY):
         scores = lax.dot_general(
             heads[k],

time: 166 us -> 166 us (level)
  no operation moved by 1% of the time
where the time goes in v2:
time: 166 us; the launch traced here: 165 us
  starting transfers between devices  63.4 us (38%)
  waiting for transfers between devices  53.2 us (32%)
  Pallas kernels  26.9 us (16%)
  local copies, waits for them, and re-layouts  7.92 us (5%)
  matrix products  6.56 us (4%)
  other arithmetic  4.89 us (3%)
  between operations  1.68 us (1%)
    ppermute x31, starting transfers between devices, shift(): return lax.ppermute(v, axis, [(i, (i + k) % n) for i in range(n)])  38.6 us
    all_to_all x5, waiting for transfers between devices, exchange(): return lax.all_to_all(v, axis, 0, 0, tiled=True)  26.7 us
    ppermute x31, waiting for transfers between devices, shift(): return lax.ppermute(v, axis, [(i, (i + k) % n) for i in range(n)])  26.5 us
    all_to_all x5, starting transfers between devices, exchange(): return lax.all_to_all(v, axis, 0, 0, tiled=True)  24.8 us
    pallas_call x1, Pallas kernels, decode(): pl.pallas_call(functools.partial(decode_kernel, width), in_specs=[pl.Bloc...  21.8 us
    pallas_call x2, Pallas kernels, core_rows(): pl.pallas_call(functools.partial(core_rows_kernel, bool(got)), in_specs=[...  5.04 us
  transfers between devices with their start and end apart: 36, of which 16 were waited for; matrix products, arithmetic and copies ran while one was open for 8% of the time, Pallas kernels for 0%

profile of v2, /device:TPU:1, one launch (start us, length us, event | category | flops | bytes accessed | tf_op | source)
XLA Modules:
  0.0 164.5 jit_solution(9808586320249780974)
XLA Ops:
  0.6 2.4 %shard_map.146 = bf16[4,8,32,512]{3,2,1,0:T(8,128)(2,1)} custom-call(s32[1]{0:T(128)} %bitcast.2.core, f32[8,4,2,32,512]{4,3,2,1,0:T(8,128)} %bitcast.56), custom_call_target="tpu_custom_call" | custom-call | tf_op jit(solution)/shard_map/pallas_call | solution.py:70
  3.0 3.3 %collective-permute-start = (bf16[4,8,32,512]{3,2,1,0:T(8,128)(2,1)}, bf16[4,8,32,512]{3,2,1,0:T(8,128)(2,1)S(1)}, u32[]{:S(2)}, u32[]{:S(2)}) collective-permute-start(bf16[4,8,32,512]{3,2,1,0:T(8,128)(2,1)} %shard_map.146), channel_id=1, source_target_pairs={{0,4},{4,0},{1,5},{5,1},{2,6},{6,2},{3,7},{7,3},{8,12},{12,8},{9,1... | collective-permute-start | bytes 3145736 | tf_op jit(solution)/shard_map/ppermute | solution.py:35
  10.1 2.7 %shard_map.147 = bf16[4,8,32,512]{3,2,1,0:T(8,128)(2,1)} custom-call(s32[1]{0:T(128)} %bitcast.core, f32[8,4,2,32,512]{4,3,2,1,0:T(8,128)} %bitcast.57, bf16[4,8,32,512]{3,2,1,0:T(8,128)(2,1)} %copy-done.2), custom_call_target="tpu_custom_call" | custom-call | tf_op jit(solution)/shard_map/pallas_call | solution.py:70
  12.8 3.7 %all-to-all-start = ((bf16[4,8,32,512]{3,2,1,0:T(8,128)(2,1)}), bf16[4,8,32,512]{3,2,1,0:T(8,128)(2,1)S(1)}, u32[]{:S(2)}, u32[]{:S(2)}) async-start(bf16[4,8,32,512]{3,2,1,0:T(8,128)(2,1)} %shard_map.147), calls=%async_computation | async-start | bytes 2097152 | tf_op jit(solution)/shard_map/all_to_all | solution.py:29
  16.6 1.6 collective-permute-start.1
  18.4 6.4 %collective-permute-done.1.refs_1_ = bf16[64,2048]{1,0:T(8,128)(2,1)} collective-permute-done((bf16[64,2048]{1,0:T(8,128)(2,1)}, bf16[64,2048]{1,0:T(8,128)(2,1)}, u32[]{:S(2)}, u32[]{:S(2)}) %collective-permute-start.1) | collective-permute-done | bytes 262176 | tf_op jit(solution)/shard_map/ppermute | solution.py:35
  24.8 2.1 %collective-permute-done.2.refs_3_ = bf16[64,2048]{1,0:T(8,128)(2,1)} collective-permute-done((bf16[64,2048]{1,0:T(8,128)(2,1)}, bf16[64,2048]{1,0:T(8,128)(2,1)}, u32[]{:S(2)}, u32[]{:S(2)}) %collective-permute-start.2) | collective-permute-done | bytes 262176 | tf_op jit(solution)/shard_map/ppermute | solution.py:35
  26.8 4.7 %all-to-all-done = bf16[4,8,32,512]{3,2,1,0:T(8,128)(2,1)S(1)} async-done(((bf16[4,8,32,512]{3,2,1,0:T(8,128)(2,1)}), bf16[4,8,32,512]{3,2,1,0:T(8,128)(2,1)S(1)}, u32[]{:S(2)}, u32[]{:S(2)}) %all-to-all-start) | async-done | bytes 1048608 | tf_op jit(solution)/shard_map/all_to_all | solution.py:29
  32.4 6.7 %all-to-all-start.1 = ((bf16[8,32,512]{2,1,0:T(8,128)(2,1)}), bf16[8,32,512]{2,1,0:T(8,128)(2,1)S(1)}, u32[]{:S(2)}, u32[]{:S(2)}) async-start(bf16[8,32,512]{2,1,0:T(8,128)(2,1)} %reduce_sum.30), calls=%async_computation.1 | async-start | bytes 524288 | tf_op jit(solution)/shard_map/all_to_all | solution.py:29
  42.6 2.9 %collective-permute-start.6 = (bf16[64,2048]{1,0:T(8,128)(2,1)}, bf16[64,2048]{1,0:T(8,128)(2,1)}, u32[]{:S(2)}, u32[]{:S(2)}) collective-permute-start(bf16[64,2048]{1,0:T(8,128)(2,1)} %bitcast.5.refs_0_), channel_id=1, source_target_pairs={{0,2},{1,3},{2,0},{3,1},{4,6},{5,7},{6,4},{7,5},{8,10},{9,11},{10,... | collective-permute-start | bytes 786440 | tf_op jit(solution)/shard_map/ppermute | solution.py:35
  45.7 3.3 %all-to-all-done.1 = bf16[8,32,512]{2,1,0:T(8,128)(2,1)S(1)} async-done(((bf16[8,32,512]{2,1,0:T(8,128)(2,1)}), bf16[8,32,512]{2,1,0:T(8,128)(2,1)S(1)}, u32[]{:S(2)}, u32[]{:S(2)}) %all-to-all-start.1) | async-done | bytes 262176 | tf_op jit(solution)/shard_map/all_to_all | solution.py:29
  51.3 3.4 %all-to-all-start.2 = ((bf16[8,32,512]{2,1,0:T(8,128)(2,1)}), bf16[8,32,512]{2,1,0:T(8,128)(2,1)S(1)}, u32[]{:S(2)}, u32[]{:S(2)}) async-start(bf16[8,32,512]{2,1,0:T(8,128)(2,1)} %broadcast_in_dim.14), calls=%async_computation.2 | async-start | bytes 524288 | tf_op jit(solution)/shard_map/all_to_all | solution.py:29
  55.6 2.7 %convolution_convert_fusion = bf16[256,2176]{1,0:T(8,128)(2,1)} fusion(bf16[48,2176]{1,0:T(8,128)(2,1)} %collective-permute-done.5, bf16[48,2176]{1,0:T(8,128)(2,1)} %collective-permute-done.4, bf16[48,2176]{1,0:T(8,128)(2,1)} %collective-permute-done.3, bf16[48,2176]{1,0:T(8,128)(2,1)S(1)} %get-tuple-element.61, s32[256]{0:T(256)S(1)} %compare_select_fusion.4), kind=kOutput, calls=%fused_computation.2 | convolution fusion | flops 217858048 | bytes 1950720 | tf_op jit(solution)/shard_map/dot_general | solution.py:288
  58.2 5.8 %all-to-all-done.2 = bf16[8,32,512]{2,1,0:T(8,128)(2,1)S(1)} async-done(((bf16[8,32,512]{2,1,0:T(8,128)(2,1)}), bf16[8,32,512]{2,1,0:T(8,128)(2,1)S(1)}, u32[]{:S(2)}, u32[]{:S(2)}) %all-to-all-start.2) | async-done | bytes 262176 | tf_op jit(solution)/shard_map/all_to_all | solution.py:29
  64.0 7.5 %all-to-all-start.3 = ((bf16[16,16,2176]{2,1,0:T(8,128)(2,1)}), bf16[16,16,2176]{2,1,0:T(8,128)(2,1)S(1)}, u32[]{:S(2)}, u32[]{:S(2)}) async-start(bf16[16,16,2176]{2,1,0:T(8,128)(2,1)} %bitcast.10), calls=%async_computation.3 | async-start | bytes 2228224 | tf_op jit(solution)/shard_map/all_to_all | solution.py:29
  71.6 3.0 %collective-permute-start.9 = (bf16[8,32,256]{2,1,0:T(8,128)(2,1)S(1)}, bf16[8,32,256]{2,1,0:T(8,128)(2,1)S(1)}, u32[]{:S(2)}, u32[]{:S(2)}) collective-permute-start(bf16[8,32,256]{2,1,0:T(8,128)(2,1)S(1)} %get-tuple-element.68), channel_id=1, source_target_pairs={{0,24},{8,0},{16,8},{24,16},{1,25},{9,1},{17,9},{25,17},{2,26},{10... | collective-permute-start | bytes 393224 | tf_op jit(solution)/shard_map/ppermute | solution.py:35
  78.0 2.0 %collective-permute-done.9 = bf16[8,32,256]{2,1,0:T(8,128)(2,1)S(1)} collective-permute-done((bf16[8,32,256]{2,1,0:T(8,128)(2,1)S(1)}, bf16[8,32,256]{2,1,0:T(8,128)(2,1)S(1)}, u32[]{:S(2)}, u32[]{:S(2)}) %collective-permute-start.9) | collective-permute-done | bytes 131104 | tf_op jit(solution)/shard_map/ppermute | solution.py:35
  80.7 3.7 %collective-permute-done.7 = bf16[8,32,256]{2,1,0:T(8,128)(2,1)S(1)} collective-permute-done((bf16[8,32,256]{2,1,0:T(8,128)(2,1)S(1)}, bf16[8,32,256]{2,1,0:T(8,128)(2,1)S(1)}, u32[]{:S(2)}, u32[]{:S(2)}) %collective-permute-start.7) | collective-permute-done | bytes 131104 | tf_op jit(solution)/shard_map/ppermute | solution.py:35
  84.5 2.1 %collective-permute-done.10 = bf16[8,32,256]{2,1,0:T(8,128)(2,1)S(1)} collective-permute-done((bf16[8,32,256]{2,1,0:T(8,128)(2,1)S(1)}, bf16[8,32,256]{2,1,0:T(8,128)(2,1)S(1)}, u32[]{:S(2)}, u32[]{:S(2)}) %collective-permute-start.10) | collective-permute-done | bytes 131104 | tf_op jit(solution)/shard_map/ppermute | solution.py:35
  86.7 2.7 %collective-permute-start.14 = (bf16[4,8,32,256]{3,2,1,0:T(8,128)(2,1)S(1)}, bf16[4,8,32,256]{3,2,1,0:T(8,128)(2,1)S(1)}, u32[]{:S(2)}, u32[]{:S(2)}) collective-permute-start(bf16[4,8,32,256]{3,2,1,0:T(8,128)(2,1)S(1)} %pad_maximum_fusion.refs_4_), channel_id=1, source_target_pairs={{0,3},{1,0},{2,1},{3,2},{4,7},{5,4},{6,5},{7,6},{8,11},{9,8},{10,9... | collective-permute-start | bytes 1572872 | tf_op jit(solution)/shard_map/ppermute | solution.py:35
  89.5 2.5 %collective-permute-start.16 = (bf16[4,8,32,256]{3,2,1,0:T(8,128)(2,1)S(1)}, bf16[4,8,32,256]{3,2,1,0:T(8,128)(2,1)}, u32[]{:S(2)}, u32[]{:S(2)}) collective-permute-start(bf16[4,8,32,256]{3,2,1,0:T(8,128)(2,1)S(1)} %pad_maximum_fusion.1.refs_14_), channel_id=1, source_target_pairs={{0,24},{8,0},{16,8},{24,16},{1,25},{9,1},{17,9},{25,17},{2,26},{10... | collective-permute-start | bytes 1572872 | tf_op jit(solution)/shard_map/ppermute | solution.py:35
  92.1 2.4 %collective-permute-start.21 = (bf16[4,8,32,256]{3,2,1,0:T(8,128)(2,1)S(1)}, bf16[4,8,32,256]{3,2,1,0:T(8,128)(2,1)S(1)}, u32[]{:S(2)}, u32[]{:S(2)}) collective-permute-start(bf16[4,8,32,256]{3,2,1,0:T(8,128)(2,1)S(1)} %pad_maximum_fusion.refs_4_), channel_id=1, source_target_pairs={{0,4},{4,0},{1,5},{5,1},{2,6},{6,2},{3,7},{7,3},{8,12},{12,8},{9,1... | collective-permute-start | bytes 1572872 | tf_op jit(solution)/shard_map/ppermute | solution.py:35
  94.5 5.6 %collective-permute-done.13.refs_6_ = bf16[4,8,32,256]{3,2,1,0:T(8,128)(2,1)S(1)} collective-permute-done((bf16[4,8,32,256]{3,2,1,0:T(8,128)(2,1)S(1)}, bf16[4,8,32,256]{3,2,1,0:T(8,128)(2,1)S(1)}, u32[]{:S(2)}, u32[]{:S(2)}) %collective-permute-start.13) | collective-permute-done | bytes 524320 | tf_op jit(solution)/shard_map/ppermute | solution.py:35
  100.2 2.1 %collective-permute-done.15.refs_16_ = bf16[4,8,32,256]{3,2,1,0:T(8,128)(2,1)} collective-permute-done((bf16[4,8,32,256]{3,2,1,0:T(8,128)(2,1)S(1)}, bf16[4,8,32,256]{3,2,1,0:T(8,128)(2,1)}, u32[]{:S(2)}, u32[]{:S(2)}) %collective-permute-start.15) | collective-permute-done | bytes 524320 | tf_op jit(solution)/shard_map/ppermute | solution.py:35
  102.4 2.7 %collective-permute-start.18 = (bf16[2,8,32,256]{3,2,1,0:T(8,128)(2,1)S(1)}, bf16[2,8,32,256]{3,2,1,0:T(8,128)(2,1)S(1)}, u32[]{:S(2)}, u32[]{:S(2)}) collective-permute-start(bf16[2,8,32,256]{3,2,1,0:T(8,128)(2,1)S(1)} %slice.48), channel_id=1, source_target_pairs={{0,3},{1,0},{2,1},{3,2},{4,7},{5,4},{6,5},{7,6},{8,11},{9,8},{10,9... | collective-permute-start | bytes 786440 | tf_op jit(solution)/shard_map/ppermute | solution.py:35
  107.3 2.6 %collective-permute-start.20 = (bf16[2,8,32,256]{3,2,1,0:T(8,128)(2,1)S(1)}, bf16[2,8,32,256]{3,2,1,0:T(8,128)(2,1)S(1)}, u32[]{:S(2)}, u32[]{:S(2)}) collective-permute-start(bf16[2,8,32,256]{3,2,1,0:T(8,128)(2,1)S(1)} %slice.50), channel_id=1, source_target_pairs={{0,24},{8,0},{16,8},{24,16},{1,25},{9,1},{17,9},{25,17},{2,26},{10... | collective-permute-start | bytes 786440 | tf_op jit(solution)/shard_map/ppermute | solution.py:35
  109.9 3.9 %collective-permute-start.26 = (bf16[4,8,32,256]{3,2,1,0:T(8,128)(2,1)S(1)}, bf16[4,8,32,256]{3,2,1,0:T(8,128)(2,1)}, u32[]{:S(2)}, u32[]{:S(2)}) collective-permute-start(bf16[4,8,32,256]{3,2,1,0:T(8,128)(2,1)S(1)} %pad_maximum_fusion.1.refs_14_), channel_id=1, source_target_pairs={{0,4},{4,0},{1,5},{5,1},{2,6},{6,2},{3,7},{7,3},{8,12},{12,8},{9,1... | collective-permute-start | bytes 1572872 | tf_op jit(solution)/shard_map/ppermute | solution.py:35
  114.4 2.8 %collective-permute-start.27 = (bf16[4,8,32,256]{3,2,1,0:T(8,128)(2,1)}, bf16[4,8,32,256]{3,2,1,0:T(8,128)(2,1)}, u32[]{:S(2)}, u32[]{:S(2)}) collective-permute-start(bf16[4,8,32,256]{3,2,1,0:T(8,128)(2,1)} %collective-permute-done.15.refs_16_), channel_id=1, source_target_pairs={{0,4},{4,0},{1,5},{5,1},{2,6},{6,2},{3,7},{7,3},{8,12},{12,8},{9,1... | collective-permute-start | bytes 1572872 | tf_op jit(solution)/shard_map/ppermute | solution.py:35
  123.5 21.8 %shard_map.148 = bf16[4,208,512]{2,1,0:T(8,128)(2,1)} custom-call(s32[4]{0:T(128)} %pad_add_fusion.place, bf16[192,2176]{1,0:T(8,128)(2,1)} %convolution_convert_fusion.1.slots_ref, bf16[128,2176]{1,0:T(8,128)(2,1)} %constant_dynamic-slice_fusion.envs_ref, bf16[256,2048]{1,0:T(8,128)(2,1)} %table_from.1, f32[1,2048]{1,0:T(1,128)} %bitcast.72, ...), custom_call_target="tpu_custom_call" | custom-call | flops 10737418240 | bytes 8388608 | tf_op jit(solution)/shard_map/pallas_call | solution.py:199
  145.3 3.5 %all-to-all-start.4 = ((bf16[4,208,512]{2,1,0:T(8,128)(2,1)}), bf16[4,208,512]{2,1,0:T(8,128)(2,1)S(1)}, u32[]{:S(2)}, u32[]{:S(2)}) async-start(bf16[4,208,512]{2,1,0:T(8,128)(2,1)} %shard_map.148), calls=%async_computation.4 | async-start | bytes 1703936 | tf_op jit(solution)/shard_map/all_to_all | solution.py:29
  148.9 12.9 %all-to-all-done.4 = bf16[4,208,512]{2,1,0:T(8,128)(2,1)S(1)} async-done(((bf16[4,208,512]{2,1,0:T(8,128)(2,1)}), bf16[4,208,512]{2,1,0:T(8,128)(2,1)S(1)}, u32[]{:S(2)}, u32[]{:S(2)}) %all-to-all-start.4) | async-done | bytes 852000 | tf_op jit(solution)/shard_map/all_to_all | solution.py:29
  162.6 1.9 %fusion.3 = bf16[768,512]{1,0:T(8,128)(2,1)} fusion(bf16[832,512]{1,0:T(8,128)(2,1)S(1)} %bitcast.59, s32[768]{0:T(1024)S(1)} %fusion.34), kind=kOutput, calls=%fused_computation.8 | convolution fusion | flops 655343616 | bytes 1641472 | tf_op jit(solution)/shard_map/dot_general | solution.py:329
  (120 shorter events, 25.5 us)
Async XLA Ops:
  3.0 6.1 %collective-permute-start = (bf16[4,8,32,512]{3,2,1,0:T(8,128)(2,1)}, bf16[4,8,32,512]{3,2,1,0:T(8,128)(2,1)S(1)}, u32[]{:S(2)}, u32[]{:S(2)}) collective-permute-start(bf16[4,8,32,512]{3,2,1,0:T(8,128)(2,1)} %shard_map.146), channel_id=1, source_target_pairs={{0,4},{4,0},{1,5},{5,1},{2,6},{6,2},{3,7},{7,3},{8,12},{12,8},{9,1... | collective-permute-start | bytes 3145736 | tf_op jit(solution)/shard_map/ppermute | solution.py:35
  12.8 18.7 %all-to-all-start = ((bf16[4,8,32,512]{3,2,1,0:T(8,128)(2,1)}), bf16[4,8,32,512]{3,2,1,0:T(8,128)(2,1)S(1)}, u32[]{:S(2)}, u32[]{:S(2)}) async-start(bf16[4,8,32,512]{3,2,1,0:T(8,128)(2,1)} %shard_map.147), calls=%async_computation | async-start | bytes 2097152 | tf_op jit(solution)/shard_map/all_to_all | solution.py:29
  16.6 8.2 %collective-permute-start.1 = (bf16[64,2048]{1,0:T(8,128)(2,1)}, bf16[64,2048]{1,0:T(8,128)(2,1)}, u32[]{:S(2)}, u32[]{:S(2)}) collective-permute-start(bf16[64,2048]{1,0:T(8,128)(2,1)} %bitcast.5.refs_0_), channel_id=1, source_target_pairs={{0,3},{1,0},{2,1},{3,2},{4,7},{5,4},{6,5},{7,6},{8,11},{9,8},{10,9... | collective-permute-start | bytes 786440 | tf_op jit(solution)/shard_map/ppermute | solution.py:35
  18.2 8.7 %collective-permute-start.2 = (bf16[64,2048]{1,0:T(8,128)(2,1)}, bf16[64,2048]{1,0:T(8,128)(2,1)}, u32[]{:S(2)}, u32[]{:S(2)}) collective-permute-start(bf16[64,2048]{1,0:T(8,128)(2,1)} %bitcast.5.refs_0_), channel_id=1, source_target_pairs={{0,1},{1,2},{2,3},{3,0},{4,5},{5,6},{6,7},{7,4},{8,9},{9,10},{10,1... | collective-permute-start | bytes 786440 | tf_op jit(solution)/shard_map/ppermute | solution.py:35
  32.4 16.5 %all-to-all-start.1 = ((bf16[8,32,512]{2,1,0:T(8,128)(2,1)}), bf16[8,32,512]{2,1,0:T(8,128)(2,1)S(1)}, u32[]{:S(2)}, u32[]{:S(2)}) async-start(bf16[8,32,512]{2,1,0:T(8,128)(2,1)} %reduce_sum.30), calls=%async_computation.1 | async-start | bytes 524288 | tf_op jit(solution)/shard_map/all_to_all | solution.py:29
  40.5 15.1 %collective-permute-start.5 = (bf16[48,2176]{1,0:T(8,128)(2,1)}, bf16[48,2176]{1,0:T(8,128)(2,1)}, u32[]{:S(2)}, u32[]{:S(2)}) collective-permute-start(bf16[48,2176]{1,0:T(8,128)(2,1)} %get-tuple-element.62), channel_id=1, source_target_pairs={{0,24},{8,0},{16,8},{24,16},{1,25},{9,1},{17,9},{25,17},{2,26},{10... | collective-permute-start | bytes 626696 | tf_op jit(solution)/shard_map/ppermute | solution.py:35
  41.4 14.2 %collective-permute-start.4 = (bf16[48,2176]{1,0:T(8,128)(2,1)S(1)}, bf16[48,2176]{1,0:T(8,128)(2,1)}, u32[]{:S(2)}, u32[]{:S(2)}) collective-permute-start(bf16[48,2176]{1,0:T(8,128)(2,1)S(1)} %get-tuple-element.63), channel_id=1, source_target_pairs={{0,16},{8,24},{16,0},{24,8},{1,17},{9,25},{17,1},{25,9},{2,18},{10... | collective-permute-start | bytes 626696 | tf_op jit(solution)/shard_map/ppermute | solution.py:35
  42.6 13.0 %collective-permute-start.3 = (bf16[48,2176]{1,0:T(8,128)(2,1)S(1)}, bf16[48,2176]{1,0:T(8,128)(2,1)}, u32[]{:S(2)}, u32[]{:S(2)}) collective-permute-start(bf16[48,2176]{1,0:T(8,128)(2,1)S(1)} %get-tuple-element.64), channel_id=1, source_target_pairs={{0,8},{8,16},{16,24},{24,0},{1,9},{9,17},{17,25},{25,1},{2,10},{10... | collective-permute-start | bytes 626696 | tf_op jit(solution)/shard_map/ppermute | solution.py:35
  42.6 15.6 %collective-permute-start.6 = (bf16[64,2048]{1,0:T(8,128)(2,1)}, bf16[64,2048]{1,0:T(8,128)(2,1)}, u32[]{:S(2)}, u32[]{:S(2)}) collective-permute-start(bf16[64,2048]{1,0:T(8,128)(2,1)} %bitcast.5.refs_0_), channel_id=1, source_target_pairs={{0,2},{1,3},{2,0},{3,1},{4,6},{5,7},{6,4},{7,5},{8,10},{9,11},{10,... | collective-permute-start | bytes 786440 | tf_op jit(solution)/shard_map/ppermute | solution.py:35
  51.3 12.7 %all-to-all-start.2 = ((bf16[8,32,512]{2,1,0:T(8,128)(2,1)}), bf16[8,32,512]{2,1,0:T(8,128)(2,1)S(1)}, u32[]{:S(2)}, u32[]{:S(2)}) async-start(bf16[8,32,512]{2,1,0:T(8,128)(2,1)} %broadcast_in_dim.14), calls=%async_computation.2 | async-start | bytes 524288 | tf_op jit(solution)/shard_map/all_to_all | solution.py:29
  64.0 54.5 %all-to-all-start.3 = ((bf16[16,16,2176]{2,1,0:T(8,128)(2,1)}), bf16[16,16,2176]{2,1,0:T(8,128)(2,1)S(1)}, u32[]{:S(2)}, u32[]{:S(2)}) async-start(bf16[16,16,2176]{2,1,0:T(8,128)(2,1)} %bitcast.10), calls=%async_computation.3 | async-start | bytes 2228224 | tf_op jit(solution)/shard_map/all_to_all | solution.py:29
  71.6 8.4 %collective-permute-start.9 = (bf16[8,32,256]{2,1,0:T(8,128)(2,1)S(1)}, bf16[8,32,256]{2,1,0:T(8,128)(2,1)S(1)}, u32[]{:S(2)}, u32[]{:S(2)}) collective-permute-start(bf16[8,32,256]{2,1,0:T(8,128)(2,1)S(1)} %get-tuple-element.68), channel_id=1, source_target_pairs={{0,24},{8,0},{16,8},{24,16},{1,25},{9,1},{17,9},{25,17},{2,26},{10... | collective-permute-start | bytes 393224 | tf_op jit(solution)/shard_map/ppermute | solution.py:35
  74.6 6.1 %collective-permute-start.8 = (bf16[8,32,256]{2,1,0:T(8,128)(2,1)S(1)}, bf16[8,32,256]{2,1,0:T(8,128)(2,1)S(1)}, u32[]{:S(2)}, u32[]{:S(2)}) collective-permute-start(bf16[8,32,256]{2,1,0:T(8,128)(2,1)S(1)} %get-tuple-element.68), channel_id=1, source_target_pairs={{0,16},{8,24},{16,0},{24,8},{1,17},{9,25},{17,1},{25,9},{2,18},{10... | collective-permute-start | bytes 393224 | tf_op jit(solution)/shard_map/ppermute | solution.py:35
  75.2 9.2 %collective-permute-start.7 = (bf16[8,32,256]{2,1,0:T(8,128)(2,1)S(1)}, bf16[8,32,256]{2,1,0:T(8,128)(2,1)S(1)}, u32[]{:S(2)}, u32[]{:S(2)}) collective-permute-start(bf16[8,32,256]{2,1,0:T(8,128)(2,1)S(1)} %get-tuple-element.68), channel_id=1, source_target_pairs={{0,8},{8,16},{16,24},{24,0},{1,9},{9,17},{17,25},{25,1},{2,10},{10... | collective-permute-start | bytes 393224 | tf_op jit(solution)/shard_map/ppermute | solution.py:35
  75.8 8.7 %collective-permute-start.12 = (bf16[8,32,256]{2,1,0:T(8,128)(2,1)S(1)}, bf16[8,32,256]{2,1,0:T(8,128)(2,1)S(1)}, u32[]{:S(2)}, u32[]{:S(2)}) collective-permute-start(bf16[8,32,256]{2,1,0:T(8,128)(2,1)S(1)} %get-tuple-element.67), channel_id=1, source_target_pairs={{0,3},{1,0},{2,1},{3,2},{4,7},{5,4},{6,5},{7,6},{8,11},{9,8},{10,9... | collective-permute-start | bytes 393224 | tf_op jit(solution)/shard_map/ppermute | solution.py:35
  76.6 7.9 %collective-permute-start.11 = (bf16[8,32,256]{2,1,0:T(8,128)(2,1)S(1)}, bf16[8,32,256]{2,1,0:T(8,128)(2,1)S(1)}, u32[]{:S(2)}, u32[]{:S(2)}) collective-permute-start(bf16[8,32,256]{2,1,0:T(8,128)(2,1)S(1)} %get-tuple-element.67), channel_id=1, source_target_pairs={{0,2},{1,3},{2,0},{3,1},{4,6},{5,7},{6,4},{7,5},{8,10},{9,11},{10,... | collective-permute-start | bytes 393224 | tf_op jit(solution)/shard_map/ppermute | solution.py:35
  80.0 6.6 %collective-permute-start.10 = (bf16[8,32,256]{2,1,0:T(8,128)(2,1)S(1)}, bf16[8,32,256]{2,1,0:T(8,128)(2,1)S(1)}, u32[]{:S(2)}, u32[]{:S(2)}) collective-permute-start(bf16[8,32,256]{2,1,0:T(8,128)(2,1)S(1)} %get-tuple-element.67), channel_id=1, source_target_pairs={{0,1},{1,2},{2,3},{3,0},{4,5},{5,6},{6,7},{7,4},{8,9},{9,10},{10,1... | collective-permute-start | bytes 393224 | tf_op jit(solution)/shard_map/ppermute | solution.py:35
  86.7 13.5 %collective-permute-start.13 = (bf16[4,8,32,256]{3,2,1,0:T(8,128)(2,1)S(1)}, bf16[4,8,32,256]{3,2,1,0:T(8,128)(2,1)S(1)}, u32[]{:S(2)}, u32[]{:S(2)}) collective-permute-start(bf16[4,8,32,256]{3,2,1,0:T(8,128)(2,1)S(1)} %pad_maximum_fusion.refs_4_), channel_id=1, source_target_pairs={{0,1},{1,2},{2,3},{3,0},{4,5},{5,6},{6,7},{7,4},{8,9},{9,10},{10,1... | collective-permute-start | bytes 1572872 | tf_op jit(solution)/shard_map/ppermute | solution.py:35
  86.7 13.4 %collective-permute-start.14 = (bf16[4,8,32,256]{3,2,1,0:T(8,128)(2,1)S(1)}, bf16[4,8,32,256]{3,2,1,0:T(8,128)(2,1)S(1)}, u32[]{:S(2)}, u32[]{:S(2)}) collective-permute-start(bf16[4,8,32,256]{3,2,1,0:T(8,128)(2,1)S(1)} %pad_maximum_fusion.refs_4_), channel_id=1, source_target_pairs={{0,3},{1,0},{2,1},{3,2},{4,7},{5,4},{6,5},{7,6},{8,11},{9,8},{10,9... | collective-permute-start | bytes 1572872 | tf_op jit(solution)/shard_map/ppermute | solution.py:35
  89.4 12.9 %collective-permute-start.15 = (bf16[4,8,32,256]{3,2,1,0:T(8,128)(2,1)S(1)}, bf16[4,8,32,256]{3,2,1,0:T(8,128)(2,1)}, u32[]{:S(2)}, u32[]{:S(2)}) collective-permute-start(bf16[4,8,32,256]{3,2,1,0:T(8,128)(2,1)S(1)} %pad_maximum_fusion.1.refs_14_), channel_id=1, source_target_pairs={{0,8},{8,16},{16,24},{24,0},{1,9},{9,17},{17,25},{25,1},{2,10},{10... | collective-permute-start | bytes 1572872 | tf_op jit(solution)/shard_map/ppermute | solution.py:35
  89.5 12.7 %collective-permute-start.16 = (bf16[4,8,32,256]{3,2,1,0:T(8,128)(2,1)S(1)}, bf16[4,8,32,256]{3,2,1,0:T(8,128)(2,1)}, u32[]{:S(2)}, u32[]{:S(2)}) collective-permute-start(bf16[4,8,32,256]{3,2,1,0:T(8,128)(2,1)S(1)} %pad_maximum_fusion.1.refs_14_), channel_id=1, source_target_pairs={{0,24},{8,0},{16,8},{24,16},{1,25},{9,1},{17,9},{25,17},{2,26},{10... | collective-permute-start | bytes 1572872 | tf_op jit(solution)/shard_map/ppermute | solution.py:35
  92.1 17.8 %collective-permute-start.21 = (bf16[4,8,32,256]{3,2,1,0:T(8,128)(2,1)S(1)}, bf16[4,8,32,256]{3,2,1,0:T(8,128)(2,1)S(1)}, u32[]{:S(2)}, u32[]{:S(2)}) collective-permute-start(bf16[4,8,32,256]{3,2,1,0:T(8,128)(2,1)S(1)} %pad_maximum_fusion.refs_4_), channel_id=1, source_target_pairs={{0,4},{4,0},{1,5},{5,1},{2,6},{6,2},{3,7},{7,3},{8,12},{12,8},{9,1... | collective-permute-start | bytes 1572872 | tf_op jit(solution)/shard_map/ppermute | solution.py:35
  102.3 11.6 %collective-permute-start.17 = (bf16[2,8,32,256]{3,2,1,0:T(8,128)(2,1)S(1)}, bf16[2,8,32,256]{3,2,1,0:T(8,128)(2,1)S(1)}, u32[]{:S(2)}, u32[]{:S(2)}) collective-permute-start(bf16[2,8,32,256]{3,2,1,0:T(8,128)(2,1)S(1)} %slice.47), channel_id=1, source_target_pairs={{0,1},{1,2},{2,3},{3,0},{4,5},{5,6},{6,7},{7,4},{8,9},{9,10},{10,1... | collective-permute-start | bytes 786440 | tf_op jit(solution)/shard_map/ppermute | solution.py:35
  102.4 11.6 %collective-permute-start.18 = (bf16[2,8,32,256]{3,2,1,0:T(8,128)(2,1)S(1)}, bf16[2,8,32,256]{3,2,1,0:T(8,128)(2,1)S(1)}, u32[]{:S(2)}, u32[]{:S(2)}) collective-permute-start(bf16[2,8,32,256]{3,2,1,0:T(8,128)(2,1)S(1)} %slice.48), channel_id=1, source_target_pairs={{0,3},{1,0},{2,1},{3,2},{4,7},{5,4},{6,5},{7,6},{8,11},{9,8},{10,9... | collective-permute-start | bytes 786440 | tf_op jit(solution)/shard_map/ppermute | solution.py:35
  106.1 8.3 %collective-permute-start.19 = (bf16[2,8,32,256]{3,2,1,0:T(8,128)(2,1)S(1)}, bf16[2,8,32,256]{3,2,1,0:T(8,128)(2,1)S(1)}, u32[]{:S(2)}, u32[]{:S(2)}) collective-permute-start(bf16[2,8,32,256]{3,2,1,0:T(8,128)(2,1)S(1)} %slice.49), channel_id=1, source_target_pairs={{0,8},{8,16},{16,24},{24,0},{1,9},{9,17},{17,25},{25,1},{2,10},{10... | collective-permute-start | bytes 786440 | tf_op jit(solution)/shard_map/ppermute | solution.py:35
  107.3 9.9 %collective-permute-start.20 = (bf16[2,8,32,256]{3,2,1,0:T(8,128)(2,1)S(1)}, bf16[2,8,32,256]{3,2,1,0:T(8,128)(2,1)S(1)}, u32[]{:S(2)}, u32[]{:S(2)}) collective-permute-start(bf16[2,8,32,256]{3,2,1,0:T(8,128)(2,1)S(1)} %slice.50), channel_id=1, source_target_pairs={{0,24},{8,0},{16,8},{24,16},{1,25},{9,1},{17,9},{25,17},{2,26},{10... | collective-permute-start | bytes 786440 | tf_op jit(solution)/shard_map/ppermute | solution.py:35
  109.9 10.0 %collective-permute-start.26 = (bf16[4,8,32,256]{3,2,1,0:T(8,128)(2,1)S(1)}, bf16[4,8,32,256]{3,2,1,0:T(8,128)(2,1)}, u32[]{:S(2)}, u32[]{:S(2)}) collective-permute-start(bf16[4,8,32,256]{3,2,1,0:T(8,128)(2,1)S(1)} %pad_maximum_fusion.1.refs_14_), channel_id=1, source_target_pairs={{0,4},{4,0},{1,5},{5,1},{2,6},{6,2},{3,7},{7,3},{8,12},{12,8},{9,1... | collective-permute-start | bytes 1572872 | tf_op jit(solution)/shard_map/ppermute | solution.py:35
  113.8 6.1 %collective-permute-start.22 = (bf16[4,8,32,256]{3,2,1,0:T(8,128)(2,1)S(1)}, bf16[4,8,32,256]{3,2,1,0:T(8,128)(2,1)}, u32[]{:S(2)}, u32[]{:S(2)}) collective-permute-start(bf16[4,8,32,256]{3,2,1,0:T(8,128)(2,1)S(1)} %collective-permute-done.13.refs_6_), channel_id=1, source_target_pairs={{0,4},{4,0},{1,5},{5,1},{2,6},{6,2},{3,7},{7,3},{8,12},{12,8},{9,1... | collective-permute-start | bytes 1572872 | tf_op jit(solution)/shard_map/ppermute | solution.py:35
  114.0 6.5 %collective-permute-start.23 = (bf16[4,8,32,256]{3,2,1,0:T(8,128)(2,1)S(1)}, bf16[4,8,32,256]{3,2,1,0:T(8,128)(2,1)}, u32[]{:S(2)}, u32[]{:S(2)}) collective-permute-start(bf16[4,8,32,256]{3,2,1,0:T(8,128)(2,1)S(1)} %collective-permute-done.14.refs_8_), channel_id=1, source_target_pairs={{0,4},{4,0},{1,5},{5,1},{2,6},{6,2},{3,7},{7,3},{8,12},{12,8},{9,1... | collective-permute-start | bytes 1572872 | tf_op jit(solution)/shard_map/ppermute | solution.py:35
  114.4 6.2 %collective-permute-start.27 = (bf16[4,8,32,256]{3,2,1,0:T(8,128)(2,1)}, bf16[4,8,32,256]{3,2,1,0:T(8,128)(2,1)}, u32[]{:S(2)}, u32[]{:S(2)}) collective-permute-start(bf16[4,8,32,256]{3,2,1,0:T(8,128)(2,1)} %collective-permute-done.15.refs_16_), channel_id=1, source_target_pairs={{0,4},{4,0},{1,5},{5,1},{2,6},{6,2},{3,7},{7,3},{8,12},{12,8},{9,1... | collective-permute-start | bytes 1572872 | tf_op jit(solution)/shard_map/ppermute | solution.py:35
  117.9 3.1 %collective-permute-start.28 = (bf16[4,8,32,256]{3,2,1,0:T(8,128)(2,1)}, bf16[4,8,32,256]{3,2,1,0:T(8,128)(2,1)}, u32[]{:S(2)}, u32[]{:S(2)}) collective-permute-start(bf16[4,8,32,256]{3,2,1,0:T(8,128)(2,1)} %collective-permute-done.16.refs_18_), channel_id=1, source_target_pairs={{0,4},{4,0},{1,5},{5,1},{2,6},{6,2},{3,7},{7,3},{8,12},{12,8},{9,1... | collective-permute-start | bytes 1572872 | tf_op jit(solution)/shard_map/ppermute | solution.py:35
  145.3 16.5 %all-to-all-start.4 = ((bf16[4,208,512]{2,1,0:T(8,128)(2,1)}), bf16[4,208,512]{2,1,0:T(8,128)(2,1)S(1)}, u32[]{:S(2)}, u32[]{:S(2)}) async-start(bf16[4,208,512]{2,1,0:T(8,128)(2,1)} %shard_map.148), calls=%async_computation.4 | async-start | bytes 1703936 | tf_op jit(solution)/shard_map/all_to_all | solution.py:29
  (24 other events, 208.1 us)
